TPU v7x, 256 devices: a whole 4x4x8 slice. The times are simulated.
256 devices in a mesh: pipe: 4 (over y_lo, core), ep: 64 (over y_hi, z, x).
Axes of the slice: x: 4, y: 4 (y_hi: 2, y_lo: 2; y = y_hi * 2 + y_lo), z: 8, core: 2. Of those that a mesh axis runs over, the one named last changes fastest.
Arguments:
- forward_inputs: bfloat16 [4, 8192, 3584], P('pipe', 'ep'), may hold values from -50 to 50
- forward_routes: int32 [4, 8192, 1], P('pipe', 'ep'), may hold values from 0 to 15; in each aligned block of 128 rows (0 to 127, 128 to 255, ..., all dimensions but the last counted through in order) at most 9 rows name the same one
- forward_gates: float32 [4, 8192, 1], P('pipe', 'ep'), may hold values from 0.1 to 1
- backward_inputs: bfloat16 [4, 8192, 3584], P('pipe', 'ep'), may hold values from -50 to 50
- backward_cotangent: bfloat16 [4, 8192, 3584], P('pipe', 'ep'), may hold values from -6 to 6
- backward_routes: int32 [4, 8192, 1], P('pipe', 'ep'), may hold values from 0 to 15; in each aligned block of 128 rows (0 to 127, 128 to 255, ..., all dimensions but the last counted through in order) at most 9 rows name the same one
- backward_gates: float32 [4, 8192, 1], P('pipe', 'ep'), may hold values from 0.1 to 1
- saved_preacts: bfloat16 [4, 64, 576, 512], P('pipe', 'ep'), may hold values from -6 to 6
- norm_gain: float32 [4, 3584], P('pipe'), may hold values from 0.1 to 1.9
- gate_weight: bfloat16 [4, 3584, 16384], P('pipe', None, 'ep'), may hold values from -0.09375 to 0.09375
- up_weight: bfloat16 [4, 3584, 16384], P('pipe', None, 'ep'), may hold values from -0.09375 to 0.09375
- down_weight: bfloat16 [4, 16384, 3584], P('pipe', 'ep'), may hold values from -0.1875 to 0.1875
Outputs:
- forward_outputs: bfloat16 [4, 8192, 3584], P('pipe', 'ep')
- input_grads: bfloat16 [4, 8192, 3584], P('pipe', 'ep')
Inputs may be any that keep to these rules, and one draw needn't show every extreme that they name: `forward_routes`: each token names 1 different experts; in each section the rows of one device name any expert at most 9 times. `backward_routes`: each token names 1 different experts; in each section the rows of one device name any expert at most 9 times.
All inputs are finite; a program needn't handle non-finite values.
Results may differ from a plain program's by a relative error of at most 0.005.
Values may be sent and summed in bfloat16 or wider, within the bound.
A program may use at most 128 MiB of HBM per device.

v0:
```python
import jax
import jax.numpy as jnp
from jax import lax
from jax.sharding import PartitionSpec as P

SPLIT = 4


epsilon = 1e-06


def from_behind(value, axis, steps):
    count = lax.axis_size(axis)
    pairs = [(source, (source + steps) % count) for source in range(count)]
    return lax.ppermute(value, axis, pairs)


def device_routes(routes, split):
    widened = routes[:, :, None] * split + jnp.arange(split, dtype=jnp.int32)[None, None, :]
    return widened.reshape(routes.shape[0], -1)


def slot_rows(routes, capacity, groups):
    flattened = routes.reshape(-1)
    onehot = (flattened[:, None] == jnp.arange(groups, dtype=jnp.int32)[None, :]).astype(jnp.int32)
    before = jnp.cumsum(onehot, axis=0) - onehot
    return flattened * capacity + jnp.sum(onehot * before, axis=1)


def pack_rows(slot_index, values, weights, capacity, groups, node_count):
    slot_total = groups * capacity
    pair_count = slot_index.shape[0]
    matches = slot_index[None, :] == jnp.arange(slot_total, dtype=jnp.int32)[:, None]
    filled = jnp.any(matches, axis=1)
    source = jnp.sum(
        jnp.where(matches, jnp.arange(pair_count, dtype=jnp.int32)[None, :], 0), axis=1
    )
    token_index = jnp.where(filled, source // node_count, values.shape[0])
    padded_values = jnp.concatenate((values, jnp.zeros((1, values.shape[1]), values.dtype)), 0)
    picked = padded_values[token_index]
    weight_rows = weights.reshape(pair_count, -1)
    padded_weights = jnp.concatenate(
        (weight_rows, jnp.zeros((1, weight_rows.shape[1]), weights.dtype)), 0
    )
    pair_index = jnp.where(filled, source, pair_count)
    picked_weights = padded_weights[pair_index]
    return (picked.reshape(groups, capacity, -1), picked_weights.reshape(groups, capacity, -1))


def gather_pairs(results, slot_index, token_count, node_count):
    flat_rows = results.reshape(-1, results.shape[-1])
    index_grid = slot_index.reshape(token_count, node_count)
    total = flat_rows[index_grid[:, 0]].astype(jnp.float32)
    for member in range(1, node_count):
        total = total + flat_rows[index_grid[:, member]].astype(jnp.float32)
    return total


def unit_rows(values, gain_row):
    widened = values.astype(jnp.float32)
    inverse = lax.rsqrt(jnp.mean(widened * widened, axis=-1, keepdims=True) + epsilon)
    return (widened * inverse * gain_row[None, :]).astype(jnp.bfloat16)


def experts_forward(rows_in, weights_in, joined, down_local):
    hidden_width = down_local.shape[0]
    preacts = jnp.dot(rows_in, joined, preferred_element_type=jnp.float32)
    pre_gate = preacts[:, :hidden_width]
    pre_up = preacts[:, hidden_width:]
    hidden = (weights_in.astype(jnp.float32) * jax.nn.silu(pre_gate) * pre_up).astype(jnp.bfloat16)
    return jnp.dot(hidden, down_local, preferred_element_type=jnp.float32).astype(jnp.bfloat16)


def experts_backward(rows_in, weights_in, saved_rows, joined, down_local):
    hidden_width = down_local.shape[0]
    back_hidden = lax.dot_general(
        rows_in, down_local, (((1,), (1,)), ((), ())), preferred_element_type=jnp.float32
    )
    grad_hidden = weights_in.astype(jnp.float32) * back_hidden
    preacts = saved_rows.astype(jnp.float32)
    pre_gate = preacts[:, :hidden_width]
    pre_up = preacts[:, hidden_width:]
    sigmoid = jax.nn.sigmoid(pre_gate)
    grad_gate = (grad_hidden * pre_up * sigmoid * (1.0 + pre_gate * (1.0 - sigmoid))).astype(
        jnp.bfloat16
    )
    grad_up = (grad_hidden * pre_gate * sigmoid).astype(jnp.bfloat16)
    grad_joined = jnp.concatenate((grad_gate, grad_up), axis=1)
    summed = lax.dot_general(
        grad_joined, joined, (((1,), (1,)), ((), ())), preferred_element_type=jnp.float32
    )
    return summed.astype(jnp.bfloat16)


def norm_backward(kept_inputs, gain_row, grad_normed, returning):
    widened = kept_inputs.astype(jnp.float32)
    inverse = lax.rsqrt(jnp.mean(widened * widened, axis=-1, keepdims=True) + epsilon)
    normal_rows = widened * inverse
    scaled_grad = grad_normed * gain_row[None, :]
    inner_mean = jnp.mean(scaled_grad * normal_rows, axis=-1, keepdims=True)
    return (
        returning.astype(jnp.float32) + inverse * (scaled_grad - normal_rows * inner_mean)
    ).astype(jnp.bfloat16)


def on_device(
    forward_inputs,
    forward_routes,
    forward_gates,
    backward_inputs,
    backward_cotangent,
    backward_routes,
    backward_gates,
    saved_preacts,
    norm_gain,
    gate_weight,
    up_weight,
    down_weight,
):
    groups = lax.axis_size("ep")
    feature_width = forward_inputs.shape[2]
    token_count = forward_inputs.shape[1]
    node_count = forward_routes.shape[2]
    pair_count = node_count * SPLIT
    capacity = saved_preacts.shape[2] // groups
    arriving = from_behind(forward_inputs, "pipe", 1)[0]
    returning = from_behind(backward_cotangent, "pipe", -1)[0]
    gain_row = norm_gain[0]
    joined = jnp.concatenate((gate_weight[0], up_weight[0]), axis=1)
    down_local = down_weight[0]
    saved_rows = saved_preacts[0, 0]
    normed = unit_rows(arriving, gain_row)
    slots_f = slot_rows(device_routes(forward_routes[0], SPLIT), capacity, groups)
    gates_wide_f = jnp.repeat(forward_gates[0].astype(jnp.bfloat16), SPLIT, axis=1)
    send_rows_f, send_weights_f = pack_rows(
        slots_f, normed, gates_wide_f, capacity, groups, pair_count
    )
    slots_b = slot_rows(device_routes(backward_routes[0], SPLIT), capacity, groups)
    gates_wide_b = jnp.repeat(backward_gates[0].astype(jnp.bfloat16), SPLIT, axis=1)
    send_rows_b, send_weights_b = pack_rows(
        slots_b, returning, gates_wide_b, capacity, groups, pair_count
    )
    rows_in = lax.all_to_all(send_rows_f, "ep", split_axis=0, concat_axis=0, tiled=True)
    weights_in = lax.all_to_all(send_weights_f, "ep", split_axis=0, concat_axis=0, tiled=True)
    item_count = rows_in.shape[1]
    produced = experts_forward(
        rows_in.reshape(-1, feature_width), weights_in.reshape(-1, 1), joined, down_local
    )
    back_f = lax.all_to_all(
        produced.reshape(groups, item_count, feature_width),
        "ep",
        split_axis=0,
        concat_axis=0,
        tiled=True,
    )
    recv_rows_b, recv_weights_b = (
        lax.all_to_all(send_rows_b, "ep", split_axis=0, concat_axis=0, tiled=True),
        lax.all_to_all(send_weights_b, "ep", split_axis=0, concat_axis=0, tiled=True),
    )
    grad_slots = experts_backward(
        recv_rows_b.reshape(-1, feature_width),
        recv_weights_b.reshape(-1, 1),
        saved_rows,
        joined,
        down_local,
    )
    back_b = lax.all_to_all(
        grad_slots.reshape(groups, capacity, feature_width),
        "ep",
        split_axis=0,
        concat_axis=0,
        tiled=True,
    )
    expert_sum = gather_pairs(back_f, slots_f, token_count, pair_count)
    grad_normed = gather_pairs(back_b, slots_b, token_count, pair_count)
    outputs = (arriving.astype(jnp.float32) + expert_sum).astype(jnp.bfloat16)
    input_grad = norm_backward(backward_inputs[0], gain_row, grad_normed, returning)
    return (outputs[None], input_grad[None])


def solution(mesh):
    in_specs = (
        P("pipe", "ep", None),
        P("pipe", "ep", None),
        P("pipe", "ep", None),
        P("pipe", "ep", None),
        P("pipe", "ep", None),
        P("pipe", "ep", None),
        P("pipe", "ep", None),
        P("pipe", "ep", None, None),
        P("pipe", None),
        P("pipe", None, "ep"),
        P("pipe", None, "ep"),
        P("pipe", "ep", None),
    )
    out_specs = (P("pipe", "ep", None), P("pipe", "ep", None))
    return jax.shard_map(
        on_device, mesh=mesh, in_specs=in_specs, out_specs=out_specs, check_vma=False
    )
```

profile of v0, /device:TPU:1, one launch (start us, length us, event | category | flops | bytes accessed | tf_op | source)
XLA Modules:
  0.0 865.1 jit_solution(5373875959385203169)
XLA Ops:
  13.5 12.5 %all-to-all-start.3 = ((bf16[64,9,1]{1,2,0:T(2,128)(2,1)}), bf16[64,9,1]{1,2,0:T(2,128)(2,1)S(1)}, u32[]{:S(2)}, u32[]{:S(2)}) async-start(bf16[64,9,1]{1,2,0:T(2,128)(2,1)} %reshape.656), calls=%async_computation.3 | async-start | bytes 65536 | tf_op jit(solution)/shard_map/all_to_all | solution.py:158
  33.2 7.6 reshape.544
  40.9 12.5 %all-to-all-start.4 = ((bf16[64,9,3584]{2,1,0:T(8,128)(2,1)}), bf16[64,9,3584]{2,1,0:T(8,128)(2,1)}, u32[]{:S(2)}, u32[]{:S(2)}) async-start(bf16[64,9,3584]{2,1,0:T(8,128)(2,1)} %reshape.544), calls=%async_computation.4 | async-start | bytes 14680064 | tf_op jit(solution)/shard_map/all_to_all | solution.py:157
  54.8 157.8 %all-to-all-done.4 = bf16[64,9,3584]{2,1,0:T(8,128)(2,1)} async-done(((bf16[64,9,3584]{2,1,0:T(8,128)(2,1)}), bf16[64,9,3584]{2,1,0:T(8,128)(2,1)}, u32[]{:S(2)}, u32[]{:S(2)}) %all-to-all-start.4) | async-done | bytes 4128800 | tf_op jit(solution)/shard_map/all_to_all | solution.py:157
  212.6 8.0 reshape.545
  228.7 7.6 reshape.546
  236.3 11.4 %all-to-all-start.5 = ((bf16[64,9,3584]{2,1,0:T(8,128)(2,1)}), bf16[64,9,3584]{2,1,0:T(8,128)(2,1)}, u32[]{:S(2)}, u32[]{:S(2)}) async-start(bf16[64,9,3584]{2,1,0:T(8,128)(2,1)} %reshape.546), calls=%async_computation.5 | async-start | bytes 14680064 | tf_op jit(solution)/shard_map/all_to_all | solution.py:167
  257.6 22.4 %collective-permute-done = bf16[1,128,3584]{2,1,0:T(8,128)(2,1)} collective-permute-done((bf16[1,128,3584]{2,1,0:T(8,128)(2,1)}, bf16[1,128,3584]{2,1,0:T(8,128)(2,1)}, u32[]{:S(2)}, u32[]{:S(2)}) %collective-permute-start) | collective-permute-done | bytes 917536 | tf_op jit(solution)/shard_map/ppermute | solution.py:15
  281.4 125.8 %all-to-all-done.5 = bf16[64,9,3584]{2,1,0:T(8,128)(2,1)} async-done(((bf16[64,9,3584]{2,1,0:T(8,128)(2,1)}), bf16[64,9,3584]{2,1,0:T(8,128)(2,1)}, u32[]{:S(2)}, u32[]{:S(2)}) %all-to-all-start.5) | async-done | bytes 4128800 | tf_op jit(solution)/shard_map/all_to_all | solution.py:167
  407.2 11.2 %all-to-all-start = ((bf16[64,9,1]{1,2,0:T(2,128)(2,1)}), bf16[64,9,1]{1,2,0:T(2,128)(2,1)S(1)}, u32[]{:S(2)}, u32[]{:S(2)}) async-start(bf16[64,9,1]{1,2,0:T(2,128)(2,1)} %reshape.655), calls=%async_computation | async-start | bytes 65536 | tf_op jit(solution)/shard_map/all_to_all | solution.py:144
  418.4 8.0 reshape.547
  431.2 6.0 gather_fusion.9
  437.1 5.7 gather_fusion.10
  442.8 5.6 gather_fusion.11
  456.8 7.7 reshape.538
  464.5 12.5 %all-to-all-start.1 = ((bf16[64,9,3584]{2,1,0:T(8,128)(2,1)}), bf16[64,9,3584]{2,1,0:T(8,128)(2,1)}, u32[]{:S(2)}, u32[]{:S(2)}) async-start(bf16[64,9,3584]{2,1,0:T(8,128)(2,1)} %reshape.538), calls=%async_computation.1 | async-start | bytes 14680064 | tf_op jit(solution)/shard_map/all_to_all | solution.py:143
  477.2 159.0 %all-to-all-done.1 = bf16[64,9,3584]{2,1,0:T(8,128)(2,1)} async-done(((bf16[64,9,3584]{2,1,0:T(8,128)(2,1)}), bf16[64,9,3584]{2,1,0:T(8,128)(2,1)}, u32[]{:S(2)}, u32[]{:S(2)}) %all-to-all-start.1) | async-done | bytes 4128800 | tf_op jit(solution)/shard_map/all_to_all | solution.py:143
  636.2 7.9 reshape.539
  652.9 7.6 reshape.540
  660.6 11.5 %all-to-all-start.2 = ((bf16[64,9,3584]{2,1,0:T(8,128)(2,1)}), bf16[64,9,3584]{2,1,0:T(8,128)(2,1)}, u32[]{:S(2)}, u32[]{:S(2)}) async-start(bf16[64,9,3584]{2,1,0:T(8,128)(2,1)} %reshape.540), calls=%async_computation.2 | async-start | bytes 14680064 | tf_op jit(solution)/shard_map/all_to_all | solution.py:149
  676.7 154.8 %all-to-all-done.2 = bf16[64,9,3584]{2,1,0:T(8,128)(2,1)} async-done(((bf16[64,9,3584]{2,1,0:T(8,128)(2,1)}), bf16[64,9,3584]{2,1,0:T(8,128)(2,1)}, u32[]{:S(2)}, u32[]{:S(2)}) %all-to-all-start.2) | async-done | bytes 4128800 | tf_op jit(solution)/shard_map/all_to_all | solution.py:149
  831.6 8.0 reshape.541
  844.3 5.7 gather_fusion.3
  855.6 5.6 gather_fusion.5
  (100 shorter events, 81.0 us)
Async XLA Ops:
  0.6 220.0 %copy-start = (bf16[1,256,3584]{2,1,0:T(8,128)(2,1)S(1)}, bf16[1,256,3584]{2,1,0:T(8,128)(2,1)}, u32[]{:S(2)}) copy-start(bf16[1,256,3584]{2,1,0:T(8,128)(2,1)} %param.23) | copy-start | bytes 5505028
  0.6 25.5 %collective-permute-start.1 = (bf16[1,128,3584]{2,1,0:T(8,128)(2,1)}, bf16[1,128,3584]{2,1,0:T(8,128)(2,1)S(1)}, u32[]{:S(2)}, u32[]{:S(2)}) collective-permute-start(bf16[1,128,3584]{2,1,0:T(8,128)(2,1)} %param.16), channel_id=1, source_target_pairs={{0,192},{64,0},{128,64},{192,128},{1,193},{65,1},{129,65},{193,129... | collective-permute-start | bytes 2752520 | tf_op jit(solution)/shard_map/ppermute | solution.py:15
  13.5 27.4 %all-to-all-start.3 = ((bf16[64,9,1]{1,2,0:T(2,128)(2,1)}), bf16[64,9,1]{1,2,0:T(2,128)(2,1)S(1)}, u32[]{:S(2)}, u32[]{:S(2)}) async-start(bf16[64,9,1]{1,2,0:T(2,128)(2,1)} %reshape.656), calls=%async_computation.3 | async-start | bytes 65536 | tf_op jit(solution)/shard_map/all_to_all | solution.py:158
  26.1 0.9 copy-start.4
  40.9 171.8 %all-to-all-start.4 = ((bf16[64,9,3584]{2,1,0:T(8,128)(2,1)}), bf16[64,9,3584]{2,1,0:T(8,128)(2,1)}, u32[]{:S(2)}, u32[]{:S(2)}) async-start(bf16[64,9,3584]{2,1,0:T(8,128)(2,1)} %reshape.544), calls=%async_computation.4 | async-start | bytes 14680064 | tf_op jit(solution)/shard_map/all_to_all | solution.py:157
  220.7 3.7 copy-start.6
  220.7 3.7 copy-start.7
  236.3 13.4 %copy-start.8 = (s32[1,128,1]{1,2,0:T(1,128)S(1)}, s32[1,128,1]{1,2,0:T(1,128)}, u32[]{:S(2)}) copy-start(s32[1,128,1]{1,2,0:T(1,128)} %param.13) | copy-start | bytes 1540
  236.3 170.9 %all-to-all-start.5 = ((bf16[64,9,3584]{2,1,0:T(8,128)(2,1)}), bf16[64,9,3584]{2,1,0:T(8,128)(2,1)}, u32[]{:S(2)}, u32[]{:S(2)}) async-start(bf16[64,9,3584]{2,1,0:T(8,128)(2,1)} %reshape.546), calls=%async_computation.5 | async-start | bytes 14680064 | tf_op jit(solution)/shard_map/all_to_all | solution.py:167
  247.8 9.1 %copy-start.5 = (f32[1,3584]{1,0:T(1,128)S(1)}, f32[1,3584]{1,0:T(1,128)}, u32[]{:S(2)}) copy-start(f32[1,3584]{1,0:T(1,128)} %param.20) | copy-start | bytes 43012
  247.8 9.5 %copy-start.3 = (bf16[1,128,3584]{2,1,0:T(8,128)(2,1)S(1)}, bf16[1,128,3584]{2,1,0:T(8,128)(2,1)}, u32[]{:S(2)}) copy-start(bf16[1,128,3584]{2,1,0:T(8,128)(2,1)} %param.15) | copy-start | bytes 2752516
  247.8 32.2 %collective-permute-start = (bf16[1,128,3584]{2,1,0:T(8,128)(2,1)}, bf16[1,128,3584]{2,1,0:T(8,128)(2,1)}, u32[]{:S(2)}, u32[]{:S(2)}) collective-permute-start(bf16[1,128,3584]{2,1,0:T(8,128)(2,1)} %param.12), channel_id=1, source_target_pairs={{0,64},{64,128},{128,192},{192,0},{1,65},{65,129},{129,193},{193,1... | collective-permute-start | bytes 2752520 | tf_op jit(solution)/shard_map/ppermute | solution.py:15
  407.2 57.2 %all-to-all-start = ((bf16[64,9,1]{1,2,0:T(2,128)(2,1)}), bf16[64,9,1]{1,2,0:T(2,128)(2,1)S(1)}, u32[]{:S(2)}, u32[]{:S(2)}) async-start(bf16[64,9,1]{1,2,0:T(2,128)(2,1)} %reshape.655), calls=%async_computation | async-start | bytes 65536 | tf_op jit(solution)/shard_map/all_to_all | solution.py:144
  431.1 17.3 %copy-start.1 = (bf16[128,3584]{1,0:T(8,128)(2,1)}, bf16[128,3584]{1,0:T(8,128)(2,1)S(1)}, u32[]{:S(2)}) copy-start(bf16[128,3584]{1,0:T(8,128)(2,1)S(1)} %gather_fusion.8) | copy-start | bytes 2752516
  464.5 171.7 %all-to-all-start.1 = ((bf16[64,9,3584]{2,1,0:T(8,128)(2,1)}), bf16[64,9,3584]{2,1,0:T(8,128)(2,1)}, u32[]{:S(2)}, u32[]{:S(2)}) async-start(bf16[64,9,3584]{2,1,0:T(8,128)(2,1)} %reshape.538), calls=%async_computation.1 | async-start | bytes 14680064 | tf_op jit(solution)/shard_map/all_to_all | solution.py:143
  660.5 12.0 %copy-start.2 = (bf16[128,3584]{1,0:T(8,128)(2,1)S(1)}, bf16[128,3584]{1,0:T(8,128)(2,1)}, u32[]{:S(2)}) copy-start(bf16[128,3584]{1,0:T(8,128)(2,1)} %copy-done.1) | copy-start | bytes 2752516
  660.6 171.0 %all-to-all-start.2 = ((bf16[64,9,3584]{2,1,0:T(8,128)(2,1)}), bf16[64,9,3584]{2,1,0:T(8,128)(2,1)}, u32[]{:S(2)}, u32[]{:S(2)}) async-start(bf16[64,9,3584]{2,1,0:T(8,128)(2,1)} %reshape.540), calls=%async_computation.2 | async-start | bytes 14680064 | tf_op jit(solution)/shard_map/all_to_all | solution.py:149
where the time goes:
time: 880 us; the launch traced here: 865 us
  waiting for transfers between devices  620 us (70%)
  local copies, waits for them, and re-layouts  130 us (15%)
  starting transfers between devices  76.7 us (9%)
  other arithmetic  20.6 us (2%)
  matrix products  16.8 us (2%)
    all_to_all x1, waiting for transfers between devices, on_device(): lax.all_to_all(send_rows_f, 'ep', split_axis=0, concat_axis=0, tiled=True)  159 us
    all_to_all x1, waiting for transfers between devices, on_device(): lax.all_to_all(send_rows_b, 'ep', split_axis=0, concat_axis=0, tiled=True)  158 us
    all_to_all x1, waiting for transfers between devices, on_device(): lax.all_to_all(produced.reshape(groups, item_count, feature_width), 'ep',...  155 us
    all_to_all x1, waiting for transfers between devices, on_device(): lax.all_to_all(grad_slots.reshape(groups, capacity, feature_width), 'ep',...  126 us
    gather x6, local copies, waits for them, and re-layouts, gather_pairs(): total = total + flat_rows[index_grid[:, member]].astype(jnp.float32)  34.3 us
    ppermute x2, waiting for transfers between devices, from_behind(): return lax.ppermute(value, axis, pairs)  22.4 us
  transfers between devices with their start and end apart: 8, of which 5 were waited for; matrix products, arithmetic and copies ran while one was open for 10% of the time, Pallas kernels for 0%

commit v1 on v0

v1 whole, which is shorter than its diff:
```python
import functools
import jax
import jax.numpy as jnp
from jax import lax
from jax.experimental import pallas as pl
from jax.experimental.pallas import tpu as pltpu
from jax.sharding import PartitionSpec as P


RING = 4
NEXP = 16
TOK = 128
D = 3584
HID = 256
CAP = 9
ROWS = NEXP * CAP
NCH = 2
NSUB = 7
HALF = NSUB * 128
BLK = 64
PACK = NEXP * BLK
EPS = 1e-6
MESH = pl.DeviceIdType.MESH
F32 = jnp.float32
BF16 = jnp.bfloat16


def iota(shape, dim):
    return lax.broadcasted_iota(jnp.int32, shape, dim)


def nn(a, b):
    return lax.dot_general(a, b, (((1,), (0,)), ((), ())), preferred_element_type=F32)


def nt(a, b):
    return lax.dot_general(a, b, (((1,), (1,)), ((), ())), preferred_element_type=F32)


def hot(mask):
    return jnp.where(mask, 1.0, 0.0).astype(BF16)


def slot_places(routes):
    t0, t1 = iota((TOK, TOK), 0), iota((TOK, TOK), 1)
    wide = jnp.broadcast_to(routes, (TOK, TOK)).astype(F32)
    row = jnp.sum(jnp.where(t0 == t1, wide, 0.0), axis=0, keepdims=True)
    same = wide == row
    col_before = jnp.sum(jnp.where(same & (t1 < t0), 1.0, 0.0), axis=1, keepdims=True)
    row_before = jnp.sum(jnp.where(same & (t0 < t1), 1.0, 0.0), axis=0, keepdims=True)
    col = routes.astype(F32) * BLK + col_before
    return (row * BLK + row_before).astype(jnp.int32), col.astype(jnp.int32)


def kernel(fin, cot, bin_hbm, routes_f, gates_f, routes_b, gates_b, saved_hbm, gain_ref, wg_hbm, wu_hbm, wd_hbm,
           out_f, out_b,
           arr, ret, kept, saved, wg, wu, wd, put, get_m, pack_m, unpack_m, normed, send, recv, xs, xb, hs, hf, gs,
           ghb, gj, tsend, tsum, tfin, rs_in, rs_left, rs_right, ys, gnorm,
           loc_sem, p_send, p_recv, w_send, w_recv, d_send, d_recv, a_send, a_recv, h_send, h_recv, g_send, g_recv,
           r_send, r_recv):
    p, ep = lax.axis_index("pipe"), lax.axis_index("ep")
    e, k = ep // RING, ep % RING
    right = (p, e * RING + (k + 1) % RING)
    left = (p, e * RING + (k + 3) % RING)
    opposite = (p, e * RING + (k + 2) % RING)
    after, before = ((p + 1) % 4, ep), ((p + 3) % 4, ep)
    ring = {1: right, 2: opposite, 3: left}
    pending = []

    def remote(src, dst, ssem, rsem, device):
        copy = pltpu.make_async_remote_copy(src_ref=src, dst_ref=dst, send_sem=ssem, recv_sem=rsem, device_id=device,
                                            device_id_type=MESH)
        copy.start()
        pending.append(copy)
        return copy

    loads = [pltpu.make_async_copy(a, b, loc_sem.at[i]) for i, (a, b) in enumerate(
        ((wd_hbm, wd.at[0]), (wg_hbm, wg), (wu_hbm, wu), (saved_hbm, saved), (bin_hbm, kept)))]
    for load in loads:
        load.start()

    barrier = pltpu.get_barrier_semaphore()

    def greet(d, carry):
        pl.semaphore_signal(barrier, inc=1, device_id=(p, (e + d) % NEXP * RING + k), device_id_type=MESH)
        return carry

    lax.fori_loop(1, NEXP, greet, 0)
    for device in (right, left, opposite, after, before):
        pl.semaphore_signal(barrier, inc=1, device_id=device, device_id_type=MESH)
    pl.semaphore_wait(barrier, NEXP - 1 + 5)

    pipe_f = remote(fin, arr, p_send.at[0], p_recv.at[0], after)
    pipe_b = remote(cot, ret, p_send.at[1], p_recv.at[1], before)
    HA, HB = pl.ds(0, HID // 2), pl.ds(HID // 2, HID // 2)
    w_ra = remote(wd_hbm.at[HA], wd.at[3, HA], w_send.at[0], w_recv.at[0], right)
    w_lb = remote(wd_hbm.at[HB], wd.at[1, HB], w_send.at[1], w_recv.at[1], left)
    w_rb = remote(wd_hbm.at[HB], wd.at[3, HB], w_send.at[2], w_recv.at[2], right)
    w_la = remote(wd_hbm.at[HA], wd.at[1, HA], w_send.at[3], w_recv.at[3], left)

    rows_f, cols_f = slot_places(routes_f[...])
    rows_b, cols_b = slot_places(routes_b[...])

    def put_matrix(i, places):
        def one(j, carry):
            put[i, :, pl.ds(pl.multiple_of(j * 128, 128), 128)] = hot(iota((PACK, TOK), 0) == places + j * CAP)
            return carry
        lax.fori_loop(0, NSUB, one, 0)

    def get_matrix(i, places):
        def one(j, carry):
            get_m[i, pl.ds(pl.multiple_of(j * 128, 128), 128), :] = hot(iota((TOK, PACK), 1) == places + j * CAP)
            return carry
        lax.fori_loop(0, NSUB, one, 0)

    def ninth(v):
        return (v * 57) >> 9

    put_matrix(0, rows_f)
    put_matrix(1, rows_b)

    def unpack_one(j, carry):
        r = iota((ROWS, PACK), 0)
        r9 = ninth(r)
        unpack_m[pl.ds(pl.multiple_of(j * ROWS, 16), ROWS), :] = hot(
            iota((ROWS, PACK), 1) == r9 * (BLK - CAP) + r + j * CAP)
        return carry
    lax.fori_loop(0, NSUB, unpack_one, 0)
    for j in range(NSUB):
        r = iota((PACK, ROWS), 1)
        r9 = ninth(r)
        pack_m[:, j * ROWS:(j + 1) * ROWS] = hot(iota((PACK, ROWS), 0) == r9 * (BLK - CAP) + r + j * CAP)

    def spread(i, c):
        s = 2 * i + c

        def one(d, carry):
            to = (e + d) % NEXP
            pltpu.make_async_remote_copy(
                src_ref=send.at[i, c, pl.ds(pl.multiple_of(to * BLK, BLK), BLK)],
                dst_ref=recv.at[i, c, pl.ds(pl.multiple_of(e * BLK, BLK), BLK)],
                send_sem=d_send.at[s], recv_sem=d_recv.at[s],
                device_id=(p, to * RING + k), device_id_type=MESH).start()
            return carry
        lax.fori_loop(1, NEXP, one, 0)
        own = pl.ds(pl.multiple_of(e * BLK, BLK), BLK)
        recv[i, c, own, :] = send[i, c, own, :]

    def whole(i, c):
        part = pl.ds(0, PACK - BLK)
        return pltpu.make_async_remote_copy(
            src_ref=send.at[i, c, part], dst_ref=recv.at[i, c, part],
            send_sem=d_send.at[2 * i + c], recv_sem=d_recv.at[2 * i + c], device_id=right, device_id_type=MESH)

    def half(c, h):
        return pl.ds((2 * c + h) * HALF, HALF)

    def col(c, h, j):
        return pl.ds(pl.multiple_of((2 * c + h) * HALF + j * 128, 128), 128)

    def dispatch(i, values):
        for c in range(NCH):
            stack = jnp.concatenate([
                jnp.concatenate([values[:, (2 * c + h) * HALF + j * 128:(2 * c + h) * HALF + (j + 1) * 128]
                                 for h in range(2)], axis=1) for j in range(NSUB)], axis=0)
            for m in range(4):
                part = pl.ds(m * 256, 256)
                send[i, c, part, :] = nn(put[i, part, :], stack).astype(BF16)
            spread(i, c)

    def unpack(i, c, target):
        def one(j, carry):
            got = nn(unpack_m[pl.ds(pl.multiple_of(j * ROWS, 16), ROWS), :], recv[i, c]).astype(BF16)
            target[:, col(c, 0, j)] = got[:, :128]
            target[:, col(c, 1, j)] = got[:, 128:]
            return carry
        lax.fori_loop(0, NSUB, one, 0)

    pipe_f.wait_recv()
    wide = arr[...].astype(F32)
    inverse = lax.rsqrt(jnp.mean(wide * wide, axis=-1, keepdims=True) + EPS)
    normed[...] = (wide * inverse * gain_ref[...]).astype(BF16)
    dispatch(0, normed)

    pipe_b.wait_recv()
    dispatch(1, ret)

    w_ra.wait_recv()
    w_f = remote(wd.at[3, HA], wd.at[2, HA], w_send.at[4], w_recv.at[4], right)
    w_lb.wait_recv()
    w_g = remote(wd.at[1, HB], wd.at[2, HB], w_send.at[5], w_recv.at[5], left)

    gathers = []
    for c in range(NCH):
        whole(0, c).wait_recv()
        unpack(0, c, xs.at[0])
        A, B = half(c, 0), half(c, 1)
        o = 6 * c
        x_ra = remote(xs.at[0, :, A], xs.at[3, :, A], a_send.at[o], a_recv.at[o], right)
        x_lb = remote(xs.at[0, :, B], xs.at[1, :, B], a_send.at[o + 1], a_recv.at[o + 1], left)
        x_rb = remote(xs.at[0, :, B], xs.at[3, :, B], a_send.at[o + 2], a_recv.at[o + 2], right)
        x_la = remote(xs.at[0, :, A], xs.at[1, :, A], a_send.at[o + 3], a_recv.at[o + 3], left)
        gathers.append((A, B, o, x_ra, x_lb, x_rb, x_la))

    for load in loads:
        load.wait()

    get_matrix(0, cols_f)
    get_matrix(1, cols_b)

    for c in range(NCH):
        whole(1, c).wait_recv()
        unpack(1, c, xb)

    def grad_hidden(r):
        return nt(xb[...], wd[r]).astype(BF16)

    def give_grad(r):
        gs[r - 1] = grad_hidden(r)
        return remote(gs.at[r - 1], ghb.at[RING - r], g_send.at[r - 1], g_recv.at[r - 1], ring[r])

    ghb[0] = grad_hidden(0)
    w_rb.wait_recv()
    g3 = give_grad(3)
    w_la.wait_recv()
    g1 = give_grad(1)

    x_fwd = []
    for A, B, o, x_ra, x_lb, x_rb, x_la in gathers:
        x_ra.wait_recv()
        x_f = remote(xs.at[3, :, A], xs.at[2, :, A], a_send.at[o + 4], a_recv.at[o + 4], right)
        x_lb.wait_recv()
        x_g = remote(xs.at[1, :, B], xs.at[2, :, B], a_send.at[o + 5], a_recv.at[o + 5], left)
        x_fwd.append((x_f, x_g))

    w_f.wait_recv()
    w_g.wait_recv()
    g2 = give_grad(2)

    def hidden(r):
        rows = xs[r]
        pre_gate = nn(rows, wg[...])
        pre_up = nn(rows, wu[...])
        return (pre_gate / (1.0 + jnp.exp(-pre_gate)) * pre_up).astype(BF16)

    def give_hidden(r):
        hs[r - 1] = hidden(r)
        return remote(hs.at[r - 1], hf.at[RING - r], h_send.at[r - 1], h_recv.at[r - 1], ring[r])

    hf[0] = hidden(0)

    def grad_group(r):
        group = (k + r) % RING
        q = iota((ROWS, NEXP * RING * CAP), 0)
        take = hot(iota((ROWS, NEXP * RING * CAP), 1) == ninth(q) * (RING - 1) * CAP + q + group * CAP)
        pre = nn(take, saved[...])
        gate, up = pre[:, :HID], pre[:, HID:]
        grad = ghb[r].astype(F32)
        sigma = 1.0 / (1.0 + jnp.exp(-gate))
        gj[r, :, :HID] = (grad * up * sigma * (1.0 + gate * (1.0 - sigma))).astype(BF16)
        gj[r, :, HID:] = (grad * gate * sigma).astype(BF16)

    grad_group(0)
    for r, copy in ((2, g2), (1, g1), (3, g3)):
        copy.wait_recv()
    for r in (2, 1, 3):
        grad_group(r)

    def partial(r, q):
        cols = pl.ds(q * HALF, HALF)
        return nt(gj[r, :, :HID], wg[cols, :]) + nt(gj[r, :, HID:], wu[cols, :])

    sums = []
    for q in range(2 * NCH):
        cols = pl.ds(q * HALF, HALF)
        near, far = (1, 3) if q % 2 == 0 else (3, 1)
        tsend[0, :, cols] = partial(2, q).astype(BF16)
        first = remote(tsend.at[0, :, cols], rs_in.at[:, cols], r_send.at[3 * q], r_recv.at[3 * q], ring[near])
        tsend[1, :, cols] = partial(far, q).astype(BF16)
        single_to = rs_right if far == 3 else rs_left
        single = remote(tsend.at[1, :, cols], single_to.at[:, cols], r_send.at[3 * q + 1], r_recv.at[3 * q + 1],
                        ring[far])
        tsend[2, :, cols] = partial(near, q).astype(BF16)
        tfin[:, cols] = partial(0, q)
        sums.append((q, cols, near, first, single))

    finals = []
    for q, cols, near, first, single in sums:
        first.wait_recv()
        tsum[:, cols] = (tsend[2, :, cols].astype(F32) + rs_in[:, cols].astype(F32)).astype(BF16)
        summed_to = rs_left if near == 1 else rs_right
        summed = remote(tsum.at[:, cols], summed_to.at[:, cols], r_send.at[3 * q + 2], r_recv.at[3 * q + 2],
                        ring[near])
        finals.append((cols, single, summed))

    for x_f, x_g in x_fwd:
        pass
    for A, B, o, x_ra, x_lb, x_rb, x_la in gathers:
        x_rb.wait_recv()
        x_la.wait_recv()
    h1 = give_hidden(1)
    h3 = give_hidden(3)
    for x_f, x_g in x_fwd:
        x_f.wait_recv()
        x_g.wait_recv()
    h2 = give_hidden(2)

    def give_back(i, c):
        for m in range(4):
            part = pl.ds(m * 256, 256)
            send[2 + i, c, part, :] = nn(pack_m[part, :], ys[i, c]).astype(BF16)
        spread(2 + i, c)

    for copy in (h1, h3, h2):
        copy.wait_recv()
    for c in range(NCH):
        for h in range(2):
            total = nn(hf[0], wd[0, :, half(c, h)])
            for r in range(1, RING):
                total = total + nn(hf[r], wd[r, :, half(c, h)])
            total = total.astype(BF16)
            for j in range(NSUB):
                ys[0, c, j * ROWS:(j + 1) * ROWS, h * 128:(h + 1) * 128] = total[:, j * 128:(j + 1) * 128]
        give_back(0, c)

    for c in range(NCH):
        for h in range(2):
            cols, single, summed = finals[2 * c + h]
            single.wait_recv()
            summed.wait_recv()
            total = tfin[:, cols] + rs_left[:, cols].astype(F32) + rs_right[:, cols].astype(F32)
            total = total.astype(BF16)
            for j in range(NSUB):
                ys[1, c, j * ROWS:(j + 1) * ROWS, h * 128:(h + 1) * 128] = total[:, j * 128:(j + 1) * 128]
        give_back(1, c)

    gate_f = gates_f[...].astype(BF16).astype(F32)
    gate_b = gates_b[...].astype(BF16).astype(F32)

    def home(i, c, use):
        def one(j, carry):
            got = nn(get_m[i, pl.ds(pl.multiple_of(j * TOK, TOK), TOK), :], recv[2 + i, c])
            use(col(c, 0, j), got[:, :128])
            use(col(c, 1, j), got[:, 128:])
            return carry
        lax.fori_loop(0, NSUB, one, 0)

    def add_forward(cols, got):
        out_f[:, cols] = (arr[:, cols].astype(F32) + gate_f * got).astype(BF16)

    for c in range(NCH):
        whole(2, c).wait_recv()
        home(0, c, add_forward)

    kept_wide = kept[...].astype(F32)
    inverse_b = lax.rsqrt(jnp.mean(kept_wide * kept_wide, axis=-1, keepdims=True) + EPS)

    def keep(cols, got):
        gnorm[:, cols] = gate_b * got * gain_ref[:, cols]

    for c in range(NCH):
        whole(3, c).wait_recv()
        home(1, c, keep)
    scaled = gnorm[...]
    xhat = kept[...].astype(F32) * inverse_b
    inner = jnp.mean(scaled * xhat, axis=-1, keepdims=True)
    out_b[...] = (ret[...].astype(F32) + inverse_b * (scaled - xhat * inner)).astype(BF16)

    for copy in pending:
        copy.wait_send()
    for i in range(4):
        for c in range(NCH):
            whole(i, c).wait_send()


def on_device(forward_inputs, forward_routes, forward_gates, backward_inputs, backward_cotangent, backward_routes,
              backward_gates, saved_preacts, norm_gain, gate_weight, up_weight, down_weight):
    vmem = pl.BlockSpec(memory_space=pltpu.VMEM)
    hbm = pl.BlockSpec(memory_space=pl.ANY)
    dma = pltpu.SemaphoreType.DMA
    out = jax.ShapeDtypeStruct((TOK, D), BF16)
    scratch = [
        pltpu.VMEM((TOK, D), BF16),
        pltpu.VMEM((TOK, D), BF16),
        pltpu.VMEM((TOK, D), BF16),
        pltpu.VMEM((RING * ROWS, 2 * HID), BF16),
        pltpu.VMEM((D, HID), BF16),
        pltpu.VMEM((D, HID), BF16),
        pltpu.VMEM((RING, HID, D), BF16),
        pltpu.VMEM((2, PACK, NSUB * TOK), BF16),
        pltpu.VMEM((2, NSUB * TOK, PACK), BF16),
        pltpu.VMEM((PACK, NSUB * ROWS), BF16),
        pltpu.VMEM((NSUB * ROWS, PACK), BF16),
        pltpu.VMEM((TOK, D), BF16),
        pltpu.VMEM((4, NCH, PACK, 256), BF16),
        pltpu.VMEM((4, NCH, PACK, 256), BF16),
        pltpu.VMEM((RING, ROWS, D), BF16),
        pltpu.VMEM((ROWS, D), BF16),
        pltpu.VMEM((RING - 1, ROWS, HID), BF16),
        pltpu.VMEM((RING, ROWS, HID), BF16),
        pltpu.VMEM((RING - 1, ROWS, HID), BF16),
        pltpu.VMEM((RING, ROWS, HID), BF16),
        pltpu.VMEM((RING, ROWS, 2 * HID), BF16),
        pltpu.VMEM((3, ROWS, D), BF16),
        pltpu.VMEM((ROWS, D), BF16),
        pltpu.VMEM((ROWS, D), F32),
        pltpu.VMEM((ROWS, D), BF16),
        pltpu.VMEM((ROWS, D), BF16),
        pltpu.VMEM((ROWS, D), BF16),
        pltpu.VMEM((2, NCH, NSUB * ROWS, 256), BF16),
        pltpu.VMEM((TOK, D), F32),
        dma((5,)), dma((2,)), dma((2,)), dma((6,)), dma((6,)), dma((8,)), dma((8,)), dma((12,)), dma((12,)),
        dma((3,)), dma((3,)), dma((3,)), dma((3,)), dma((12,)), dma((12,)),
    ]
    call = pl.pallas_call(
        kernel,
        out_shape=(out, out),
        in_specs=[hbm, hbm, hbm, vmem, vmem, vmem, vmem, hbm, vmem, hbm, hbm, hbm],
        out_specs=(vmem, vmem),
        scratch_shapes=scratch,
        compiler_params=pltpu.CompilerParams(collective_id=0, has_side_effects=True,
                                             vmem_limit_bytes=62 * 2 ** 20),
        cost_estimate=pl.CostEstimate(flops=10 ** 10, bytes_accessed=2 * 10 ** 7, transcendentals=10 ** 6),
    )
    outputs, grads = call(
        forward_inputs[0], backward_cotangent[0], backward_inputs[0], forward_routes[0], forward_gates[0],
        backward_routes[0], backward_gates[0], saved_preacts[0, 0], norm_gain, gate_weight[0], up_weight[0],
        down_weight[0])
    return outputs[None], grads[None]


def solution(mesh):
    tokens = P("pipe", "ep", None)
    in_specs = (tokens,) * 7 + (P("pipe", "ep", None, None), P("pipe", None), P("pipe", None, "ep"),
                                P("pipe", None, "ep"), tokens)
    return jax.shard_map(on_device, mesh=mesh, in_specs=in_specs, out_specs=(tokens, tokens), check_vma=False)
```

time: 880 us -> 208 us (0.24); the launches traced: 865 us -> 204 us
  waiting for transfers between devices: 620 us -> 0 us
  Pallas kernels: 0 us -> 195 us
  local copies, waits for them, and re-layouts: 130 us -> 8.69 us
  starting transfers between devices: 76.7 us -> 0 us
  other arithmetic: 20.6 us -> 0 us
  matrix products: 16.8 us -> 0 us
    all_to_all x6 -> x0, waiting for transfers between devices: 597 us -> none  [the longest x1 159 us: on_device(): lax.all_to_all(send_rows_f, 'ep', split_axis=0, concat_axis=0, tiled=True)]
    pallas_call x0 -> x1, Pallas kernels: none -> 195 us  [on_device(): call(forward_inputs[0], backward_cotangent[0], backward_inputs[0], forwar...]
    all_to_all x6 -> x0, starting transfers between devices: 71.6 us -> none  [the longest x1 12.5 us: on_device(): lax.all_to_all(send_weights_b, 'ep', split_axis=0, concat_axis=0, tiled=T...]
    reshape x10 -> x0, local copies, waits for them, and re-layouts: 64.1 us -> none  [the longest x2 16 us: gather_pairs(): flat_rows = results.reshape(-1, results.shape[-1])]
    gather x12 -> x0, local copies, waits for them, and re-layouts: 61.6 us -> none  [the longest x6 34.3 us: gather_pairs(): total = total + flat_rows[index_grid[:, member]].astype(jnp.float32)]
    ppermute x2 -> x0, waiting for transfers between devices: 22.4 us -> none  [from_behind(): return lax.ppermute(value, axis, pairs)]
    dot_general x4 -> x0, matrix products: 16.8 us -> none  [the longest x1 5.58 us: experts_forward(): preacts = jnp.dot(rows_in, joined, preferred_element_type=jnp.float32)]
    convert_element_type x9 -> x0, other arithmetic: 10.4 us -> none  [the longest x1 4.16 us: norm_backward(): return (returning.astype(jnp.float32) + inverse * (scaled_grad - normal_r...]
  transfers between devices with their start and end apart: 8 -> 0, of which waited for: 5 -> 0; matrix products, arithmetic and copies ran while one was open for 10% -> 0% of each run, Pallas kernels for 0% -> 0%
where the time goes in v1:
time: 208 us; the launch traced here: 204 us
  Pallas kernels  195 us (94%)
  local copies, waits for them, and re-layouts  8.69 us (4%)
    pallas_call x1, Pallas kernels, on_device(): call(forward_inputs[0], backward_cotangent[0], backward_inputs[0], forwar...  195 us

profile of v1, /device:TPU:1, one launch (start us, length us, event | category | flops | bytes accessed | tf_op | source)
XLA Modules:
  0.0 204.3 jit_solution(3092641630341867274)
XLA Ops:
  0.6 1.4 copy.14.routes_f
  2.0 1.4 copy.15.gates_f
  3.4 1.4 copy.16.routes_b
  4.8 1.4 copy.17.gates_b
  6.2 195.0 %shard_map.131 = (bf16[128,3584]{1,0:T(8,128)(2,1)}, bf16[128,3584]{1,0:T(8,128)(2,1)}) custom-call(bf16[128,3584]{1,0:T(8,128)(2,1)} %bitcast.22, bf16[128,3584]{1,0:T(8,128)(2,1)} %bitcast.23, bf16[128,3584]{1,0:T(8,128)(2,1)} %bitcast.24, s32[128,1]{1,0:T(8,128)} %copy.14.routes_f, f32[128,1]{1,0:T(8,128)} %copy.15.gates_f, s32[128,1]{1,0:T(8,128)} %copy.16.routes_b, ...), custom_call_target="tpu_custom_call" | custom-call | flops 10000000000 | bytes 20000000 | tf_op jit(solution)/shard_map/pallas_call | solution.py:425
  201.1 0.0 copy-start
  201.1 2.2 %copy.20 = bf16[1,128,3584]{2,1,0:T(8,128)(2,1)} copy(bf16[1,128,3584]{2,1,0:T(8,128)(2,1)} %bitcast.14) | data formatting | bytes 1835008
  203.4 0.0 copy-done
  203.4 0.9 copy.21
Async XLA Ops:
  201.1 2.3 %copy-start = (bf16[128,3584]{1,0:T(8,128)(2,1)S(1)}, bf16[128,3584]{1,0:T(8,128)(2,1)}, u32[]{:S(2)}) copy-start(bf16[128,3584]{1,0:T(8,128)(2,1)} %get-tuple-element.5) | copy-start | bytes 2752516

commit v2 on v1

v2 whole, which is shorter than its diff:
```python
import functools
import jax
import jax.numpy as jnp
from jax import lax
from jax.experimental import pallas as pl
from jax.experimental.pallas import tpu as pltpu
from jax.sharding import PartitionSpec as P


RING = 4
NEXP = 16
TOK = 128
D = 3584
HID = 256
CAP = 9
ROWS = NEXP * CAP
NCH = 2
NSUB = 7
HALF = NSUB * 128
BLK = 64
PACK = NEXP * BLK
EPS = 1e-6
MESH = pl.DeviceIdType.MESH
F32 = jnp.float32
BF16 = jnp.bfloat16


def iota(shape, dim):
    return lax.broadcasted_iota(jnp.int32, shape, dim)


def nn(a, b):
    return lax.dot_general(a, b, (((1,), (0,)), ((), ())), preferred_element_type=F32)


def nt(a, b):
    return lax.dot_general(a, b, (((1,), (1,)), ((), ())), preferred_element_type=F32)


def hot(mask):
    return jnp.where(mask, 1.0, 0.0).astype(BF16)


def as_column(row):
    t0, t1 = iota((TOK, TOK), 0), iota((TOK, TOK), 1)
    return jnp.sum(jnp.where(t0 == t1, jnp.broadcast_to(row, (TOK, TOK)), 0.0), axis=1, keepdims=True)


def slot_places(routes):
    t0, t1 = iota((TOK, TOK), 0), iota((TOK, TOK), 1)
    row = routes.astype(F32)
    column = as_column(row)
    same = column == row
    col_before = jnp.sum(jnp.where(same & (t1 < t0), 1.0, 0.0), axis=1, keepdims=True)
    row_before = jnp.sum(jnp.where(same & (t0 < t1), 1.0, 0.0), axis=0, keepdims=True)
    col = column * BLK + col_before
    return (row * BLK + row_before).astype(jnp.int32), col.astype(jnp.int32)


def kernel(fin, cot, bin_hbm, routes_f, gates_f, routes_b, gates_b, saved_hbm, gain_ref, wg_hbm, wu_hbm, wd_hbm,
           out_f, out_b,
           arr, ret, kept, saved, wg, wu, wd, put, get_m, pack_m, unpack_m, normed, send, recv, xs, xb, hs, hf, gs,
           ghb, factor, gj, tsend, tnear, tfin, rs_in, rs_left, rs_right, ys, gnorm,
           loc_sem, p_send, p_recv, w_send, w_recv, d_send, d_recv, a_send, a_recv, h_send, h_recv, g_send, g_recv,
           r_send, r_recv):
    p, ep = lax.axis_index("pipe"), lax.axis_index("ep")
    e, k = ep // RING, ep % RING
    right = (p, e * RING + (k + 1) % RING)
    left = (p, e * RING + (k + 3) % RING)
    opposite = (p, e * RING + (k + 2) % RING)
    after, before = ((p + 1) % 4, ep), ((p + 3) % 4, ep)
    ring = {1: right, 2: opposite, 3: left}
    pending = []

    def remote(src, dst, ssem, rsem, device):
        copy = pltpu.make_async_remote_copy(src_ref=src, dst_ref=dst, send_sem=ssem, recv_sem=rsem, device_id=device,
                                            device_id_type=MESH)
        copy.start()
        pending.append(copy)
        return copy

    loads = [pltpu.make_async_copy(a, b, loc_sem.at[i]) for i, (a, b) in enumerate(
        ((wd_hbm, wd.at[0]), (wg_hbm, wg), (wu_hbm, wu), (saved_hbm, saved), (bin_hbm, kept)))]
    for load in loads:
        load.start()

    barrier = pltpu.get_barrier_semaphore()

    def greet(d, carry):
        pl.semaphore_signal(barrier, inc=1, device_id=(p, (e + d) % NEXP * RING + k), device_id_type=MESH)
        return carry

    lax.fori_loop(1, NEXP, greet, 0)
    for device in (right, left, opposite, after, before):
        pl.semaphore_signal(barrier, inc=1, device_id=device, device_id_type=MESH)
    with jax.named_scope("barrier wait"):
        pl.semaphore_wait(barrier, NEXP - 1 + 5)

    pipe_f = remote(fin, arr, p_send.at[0], p_recv.at[0], after)
    HA, HB = pl.ds(0, HID // 2), pl.ds(HID // 2, HID // 2)
    w_ra = remote(wd_hbm.at[HA], wd.at[3, HA], w_send.at[0], w_recv.at[0], right)
    w_lb = remote(wd_hbm.at[HB], wd.at[1, HB], w_send.at[1], w_recv.at[1], left)
    w_rb = remote(wd_hbm.at[HB], wd.at[3, HB], w_send.at[2], w_recv.at[2], right)
    w_la = remote(wd_hbm.at[HA], wd.at[1, HA], w_send.at[3], w_recv.at[3], left)

    def put_matrix(i, places):
        def one(j, carry):
            put[i, :, pl.ds(pl.multiple_of(j * 128, 128), 128)] = hot(iota((PACK, TOK), 0) == places + j * CAP)
            return carry
        lax.fori_loop(0, NSUB, one, 0)

    def get_matrix(i, places):
        def one(j, carry):
            get_m[i, pl.ds(pl.multiple_of(j * 128, 128), 128), :] = hot(iota((TOK, PACK), 1) == places + j * CAP)
            return carry
        lax.fori_loop(0, NSUB, one, 0)

    def ninth(v):
        return (v * 57) >> 9

    def unpack_matrix():
        def one(j, carry):
            r = iota((ROWS, PACK), 0)
            unpack_m[pl.ds(pl.multiple_of(j * ROWS, 16), ROWS), :] = hot(
                iota((ROWS, PACK), 1) == ninth(r) * (BLK - CAP) + r + j * CAP)
            return carry
        lax.fori_loop(0, NSUB, one, 0)

    def pack_matrix():
        for j in range(NSUB):
            r = iota((PACK, ROWS), 1)
            pack_m[:, j * ROWS:(j + 1) * ROWS] = hot(
                iota((PACK, ROWS), 0) == ninth(r) * (BLK - CAP) + r + j * CAP)

    def spread(i, c):
        s = 2 * i + c

        def one(d, carry):
            to = (e + d) % NEXP
            pltpu.make_async_remote_copy(
                src_ref=send.at[i, c, pl.ds(pl.multiple_of(to * BLK, BLK), BLK)],
                dst_ref=recv.at[i, c, pl.ds(pl.multiple_of(e * BLK, BLK), BLK)],
                send_sem=d_send.at[s], recv_sem=d_recv.at[s],
                device_id=(p, to * RING + k), device_id_type=MESH).start()
            return carry
        lax.fori_loop(1, NEXP, one, 0)
        own = pl.ds(pl.multiple_of(e * BLK, BLK), BLK)
        recv[i, c, own, :] = send[i, c, own, :]

    def whole(i, c):
        part = pl.ds(0, PACK - BLK)
        return pltpu.make_async_remote_copy(
            src_ref=send.at[i, c, part], dst_ref=recv.at[i, c, part],
            send_sem=d_send.at[2 * i + c], recv_sem=d_recv.at[2 * i + c], device_id=right, device_id_type=MESH)

    def half(c, h):
        return pl.ds((2 * c + h) * HALF, HALF)

    def col(c, h, j):
        return pl.ds(pl.multiple_of((2 * c + h) * HALF + j * 128, 128), 128)

    def dispatch(i, values):
        for c in range(NCH):
            stack = jnp.concatenate([
                jnp.concatenate([values[:, (2 * c + h) * HALF + j * 128:(2 * c + h) * HALF + (j + 1) * 128]
                                 for h in range(2)], axis=1) for j in range(NSUB)], axis=0)
            for m in range(4):
                part = pl.ds(m * 256, 256)
                send[i, c, part, :] = nn(put[i, part, :], stack).astype(BF16)
            spread(i, c)

    def unpack(i, c, target):
        def one(j, carry):
            got = nn(unpack_m[pl.ds(pl.multiple_of(j * ROWS, 16), ROWS), :], recv[i, c]).astype(BF16)
            target[:, col(c, 0, j)] = got[:, :128]
            target[:, col(c, 1, j)] = got[:, 128:]
            return carry
        lax.fori_loop(0, NSUB, one, 0)

    def saved_factors(r):
        group = (k + r) % RING
        q = iota((ROWS, NEXP * RING * CAP), 0)
        take = hot(iota((ROWS, NEXP * RING * CAP), 1) == ninth(q) * (RING - 1) * CAP + q + group * CAP)
        pre = nn(take, saved[...])
        gate, up = pre[:, :HID], pre[:, HID:]
        sigma = 1.0 / (1.0 + jnp.exp(-gate))
        factor[r, :, :HID] = up * sigma * (1.0 + gate * (1.0 - sigma))
        factor[r, :, HID:] = gate * sigma

    rows_f, cols_f = slot_places(routes_f[...])
    rows_b, cols_b = slot_places(routes_b[...])
    put_matrix(0, rows_f)

    with jax.named_scope("pipe f wait"):
        pipe_f.wait_recv()
    pipe_b = remote(cot, ret, p_send.at[1], p_recv.at[1], before)
    wide = arr[...].astype(F32)
    inverse = lax.rsqrt(jnp.mean(wide * wide, axis=-1, keepdims=True) + EPS)
    normed[...] = (wide * inverse * gain_ref[...]).astype(BF16)
    with jax.named_scope("dispatch f"):
        dispatch(0, normed)

    put_matrix(1, rows_b)
    unpack_matrix()
    for load in loads:
        load.wait()
    with jax.named_scope("saved factors"):
        for r in range(RING):
            saved_factors(r)

    with jax.named_scope("pipe b wait"):
        pipe_b.wait_recv()
    with jax.named_scope("dispatch b"):
        dispatch(1, ret)

    with jax.named_scope("matrices"):
        pack_matrix()
        get_matrix(0, cols_f)
        get_matrix(1, cols_b)

    def gather(c):
        with jax.named_scope(f"f disp wait {c}"):
            whole(0, c).wait_recv()
        unpack(0, c, xs.at[0])
        A, B = half(c, 0), half(c, 1)
        o = 6 * c
        x_ra = remote(xs.at[0, :, A], xs.at[3, :, A], a_send.at[o], a_recv.at[o], right)
        x_lb = remote(xs.at[0, :, B], xs.at[1, :, B], a_send.at[o + 1], a_recv.at[o + 1], left)
        x_rb = remote(xs.at[0, :, B], xs.at[3, :, B], a_send.at[o + 2], a_recv.at[o + 2], right)
        x_la = remote(xs.at[0, :, A], xs.at[1, :, A], a_send.at[o + 3], a_recv.at[o + 3], left)
        return x_ra, x_lb, x_rb, x_la

    def gather_on(c, x_ra, x_lb):
        A, B = half(c, 0), half(c, 1)
        o = 6 * c
        with jax.named_scope(f"x ra wait {c}"):
            x_ra.wait_recv()
        x_f = remote(xs.at[3, :, A], xs.at[2, :, A], a_send.at[o + 4], a_recv.at[o + 4], right)
        with jax.named_scope(f"x lb wait {c}"):
            x_lb.wait_recv()
        x_g = remote(xs.at[1, :, B], xs.at[2, :, B], a_send.at[o + 5], a_recv.at[o + 5], left)
        return x_f, x_g

    def weights_on(part):
        size = HID // 4
        a, b = pl.ds(part * size, size), pl.ds(HID // 2 + part * size, size)
        o = 4 + 2 * part
        return (remote(wd.at[3, a], wd.at[2, a], w_send.at[o], w_recv.at[o], right),
                remote(wd.at[1, b], wd.at[2, b], w_send.at[o + 1], w_recv.at[o + 1], left))

    def grad_hidden(r):
        return nt(xb[...], wd[r]).astype(BF16)

    def give_grad(r):
        gs[r - 1] = grad_hidden(r)
        return remote(gs.at[r - 1], ghb.at[RING - r], g_send.at[r - 1], g_recv.at[r - 1], ring[r])

    def hidden(r):
        rows = xs[r]
        pre_gate = nn(rows, wg[...])
        pre_up = nn(rows, wu[...])
        return (pre_gate / (1.0 + jnp.exp(-pre_gate)) * pre_up).astype(BF16)

    def give_hidden(r):
        hs[r - 1] = hidden(r)
        return remote(hs.at[r - 1], hf.at[RING - r], h_send.at[r - 1], h_recv.at[r - 1], ring[r])

    gathers = [gather(c) for c in range(NCH)]
    x_fwd = [gather_on(0, *gathers[0][:2])]
    with jax.named_scope("hidden 0"):
        hf[0] = hidden(0)

    with jax.named_scope("b disp wait 0"):
        whole(1, 0).wait_recv()
    unpack(1, 0, xb)
    x_fwd.append(gather_on(1, *gathers[1][:2]))
    with jax.named_scope("wd wait"):
        w_ra.wait_recv()
        w_lb.wait_recv()
    w_on = [weights_on(0)]
    with jax.named_scope("b disp wait 1"):
        whole(1, 1).wait_recv()
    unpack(1, 1, xb)

    with jax.named_scope("wd rest wait"):
        w_rb.wait_recv()
        w_la.wait_recv()
    with jax.named_scope("gh 3 1 0"):
        g3 = give_grad(3)
        g1 = give_grad(1)
        ghb[0] = grad_hidden(0)
    with jax.named_scope("x rb la wait"):
        for x_ra, x_lb, x_rb, x_la in gathers:
            x_rb.wait_recv()
            x_la.wait_recv()
    with jax.named_scope("hidden 1 3"):
        h1 = give_hidden(1)
        h3 = give_hidden(3)
    with jax.named_scope("x fwd wait"):
        for x_f, x_g in x_fwd:
            x_f.wait_recv()
            x_g.wait_recv()
    with jax.named_scope("hidden 2"):
        h2 = give_hidden(2)
    w_on.append(weights_on(1))

    def grad_group(r):
        grad = ghb[r].astype(F32)
        gj[r, :, :HID] = (grad * factor[r, :, :HID]).astype(BF16)
        gj[r, :, HID:] = (grad * factor[r, :, HID:]).astype(BF16)

    def partial(r, q):
        cols = pl.ds(q * HALF, HALF)
        return nt(gj[r, :, :HID], wg[cols, :]) + nt(gj[r, :, HID:], wu[cols, :])

    quarters = [pl.ds(q * HALF, HALF) for q in range(2 * NCH)]
    near = [1 if q % 2 == 0 else 3 for q in range(2 * NCH)]
    arrived = {1: rs_left, 3: rs_right}

    def send_single(q):
        cols, far = quarters[q], 4 - near[q]
        tsend[1, :, cols] = partial(far, q).astype(BF16)
        return remote(tsend.at[1, :, cols], arrived[far].at[:, cols], r_send.at[3 * q], r_recv.at[3 * q], ring[far])

    def send_first(q):
        cols = quarters[q]
        tsend[0, :, cols] = partial(2, q).astype(BF16)
        return remote(tsend.at[0, :, cols], rs_in.at[:, cols], r_send.at[3 * q + 1], r_recv.at[3 * q + 1],
                      ring[near[q]])

    def own_parts(q):
        cols = quarters[q]
        tnear[:, cols] = partial(near[q], q)
        tfin[:, cols] = partial(0, q)

    def send_sum(q, first):
        cols = quarters[q]
        with jax.named_scope(f"rs first wait {q}"):
            first.wait_recv()
        tsend[2, :, cols] = (tnear[:, cols] + rs_in[:, cols].astype(F32)).astype(BF16)
        return remote(tsend.at[2, :, cols], arrived[near[q]].at[:, cols], r_send.at[3 * q + 2],
                      r_recv.at[3 * q + 2], ring[near[q]])

    def give_back(i, c):
        for m in range(4):
            part = pl.ds(m * 256, 256)
            send[2 + i, c, part, :] = nn(pack_m[part, :], ys[i, c]).astype(BF16)
        spread(2 + i, c)

    def stack_up(i, c, h, total):
        total = total.astype(BF16)
        for j in range(NSUB):
            ys[i, c, j * ROWS:(j + 1) * ROWS, h * 128:(h + 1) * 128] = total[:, j * 128:(j + 1) * 128]

    with jax.named_scope("gh 1 3 wait"):
        g1.wait_recv()
        g3.wait_recv()
    with jax.named_scope("singles 01"):
        for r in (1, 3, 0):
            grad_group(r)
        singles = [send_single(0), send_single(1)]
    with jax.named_scope("wd on wait"):
        for pair in w_on:
            for copy in pair:
                copy.wait_recv()
    with jax.named_scope("gh 2"):
        g2 = give_grad(2)
    with jax.named_scope("singles 23"):
        singles += [send_single(2), send_single(3)]

    with jax.named_scope("h wait"):
        for copy in (h1, h3, h2):
            copy.wait_recv()
    for c in range(NCH):
        with jax.named_scope(f"out f {c}"):
            for h in range(2):
                total = nn(hf[0], wd[0, :, half(c, h)])
                for r in range(1, RING):
                    total = total + nn(hf[r], wd[r, :, half(c, h)])
                stack_up(0, c, h, total)
            give_back(0, c)

    with jax.named_scope("gh 2 wait"):
        g2.wait_recv()
    with jax.named_scope("firsts"):
        grad_group(2)
        firsts = [send_first(0), send_first(1), send_first(2)]
        own_parts(0)
        own_parts(1)
    summed = [send_sum(0, firsts[0]), send_sum(1, firsts[1])]
    with jax.named_scope("first 3"):
        firsts.append(send_first(3))
        own_parts(2)
        own_parts(3)
    summed += [send_sum(2, firsts[2]), send_sum(3, firsts[3])]

    gate_f = as_column(gates_f[...].astype(BF16).astype(F32))
    gate_b = as_column(gates_b[...].astype(BF16).astype(F32))

    def home(i, c, use):
        def one(j, carry):
            got = nn(get_m[i, pl.ds(pl.multiple_of(j * TOK, TOK), TOK), :], recv[2 + i, c])
            use(col(c, 0, j), got[:, :128])
            use(col(c, 1, j), got[:, 128:])
            return carry
        lax.fori_loop(0, NSUB, one, 0)

    def add_forward(cols, got):
        out_f[:, cols] = (arr[:, cols].astype(F32) + gate_f * got).astype(BF16)

    def home_forward(c):
        with jax.named_scope(f"home f wait {c}"):
            whole(2, c).wait_recv()
        home(0, c, add_forward)

    def finish_sums(c):
        for h in range(2):
            q = 2 * c + h
            cols = quarters[q]
            with jax.named_scope(f"rs final wait {q}"):
                singles[q].wait_recv()
                summed[q].wait_recv()
            stack_up(1, c, h, tfin[:, cols] + rs_left[:, cols].astype(F32) + rs_right[:, cols].astype(F32))
        with jax.named_scope(f"give back b {c}"):
            give_back(1, c)

    kept_wide = kept[...].astype(F32)
    inverse_b = lax.rsqrt(jnp.mean(kept_wide * kept_wide, axis=-1, keepdims=True) + EPS)

    def keep(cols, got):
        gnorm[:, cols] = gate_b * got * gain_ref[:, cols]

    home_forward(0)
    finish_sums(0)
    home_forward(1)
    finish_sums(1)

    for c in range(NCH):
        with jax.named_scope(f"home b wait {c}"):
            whole(3, c).wait_recv()
        home(1, c, keep)
    with jax.named_scope("final"):
        scaled = gnorm[...]
        xhat = kept[...].astype(F32) * inverse_b
        inner = jnp.mean(scaled * xhat, axis=-1, keepdims=True)
        out_b[...] = (ret[...].astype(F32) + inverse_b * (scaled - xhat * inner)).astype(BF16)

    for copy in pending:
        copy.wait_send()
    for i in range(4):
        for c in range(NCH):
            whole(i, c).wait_send()


def on_device(forward_inputs, forward_routes, forward_gates, backward_inputs, backward_cotangent, backward_routes,
              backward_gates, saved_preacts, norm_gain, gate_weight, up_weight, down_weight):
    vmem = pl.BlockSpec(memory_space=pltpu.VMEM)
    hbm = pl.BlockSpec(memory_space=pl.ANY)
    dma = pltpu.SemaphoreType.DMA
    out = jax.ShapeDtypeStruct((TOK, D), BF16)
    scratch = [
        pltpu.VMEM((TOK, D), BF16),
        pltpu.VMEM((TOK, D), BF16),
        pltpu.VMEM((TOK, D), BF16),
        pltpu.VMEM((RING * ROWS, 2 * HID), BF16),
        pltpu.VMEM((D, HID), BF16),
        pltpu.VMEM((D, HID), BF16),
        pltpu.VMEM((RING, HID, D), BF16),
        pltpu.VMEM((2, PACK, NSUB * TOK), BF16),
        pltpu.VMEM((2, NSUB * TOK, PACK), BF16),
        pltpu.VMEM((PACK, NSUB * ROWS), BF16),
        pltpu.VMEM((NSUB * ROWS, PACK), BF16),
        pltpu.VMEM((TOK, D), BF16),
        pltpu.VMEM((4, NCH, PACK, 256), BF16),
        pltpu.VMEM((4, NCH, PACK, 256), BF16),
        pltpu.VMEM((RING, ROWS, D), BF16),
        pltpu.VMEM((ROWS, D), BF16),
        pltpu.VMEM((RING - 1, ROWS, HID), BF16),
        pltpu.VMEM((RING, ROWS, HID), BF16),
        pltpu.VMEM((RING - 1, ROWS, HID), BF16),
        pltpu.VMEM((RING, ROWS, HID), BF16),
        pltpu.VMEM((RING, ROWS, 2 * HID), F32),
        pltpu.VMEM((RING, ROWS, 2 * HID), BF16),
        pltpu.VMEM((3, ROWS, D), BF16),
        pltpu.VMEM((ROWS, D), F32),
        pltpu.VMEM((ROWS, D), F32),
        pltpu.VMEM((ROWS, D), BF16),
        pltpu.VMEM((ROWS, D), BF16),
        pltpu.VMEM((ROWS, D), BF16),
        pltpu.VMEM((2, NCH, NSUB * ROWS, 256), BF16),
        pltpu.VMEM((TOK, D), F32),
        dma((5,)), dma((2,)), dma((2,)), dma((8,)), dma((8,)), dma((8,)), dma((8,)), dma((12,)), dma((12,)),
        dma((3,)), dma((3,)), dma((3,)), dma((3,)), dma((12,)), dma((12,)),
    ]
    call = pl.pallas_call(
        kernel,
        out_shape=(out, out),
        in_specs=[hbm, hbm, hbm, vmem, vmem, vmem, vmem, hbm, vmem, hbm, hbm, hbm],
        out_specs=(vmem, vmem),
        scratch_shapes=scratch,
        compiler_params=pltpu.CompilerParams(collective_id=0, has_side_effects=True,
                                             vmem_limit_bytes=62 * 2 ** 20),
        cost_estimate=pl.CostEstimate(flops=10 ** 10, bytes_accessed=2 * 10 ** 7, transcendentals=10 ** 6),
    )

    def row(values):
        return values.reshape(1, TOK)

    outputs, grads = call(
        forward_inputs[0], backward_cotangent[0], backward_inputs[0], row(forward_routes), row(forward_gates),
        row(backward_routes), row(backward_gates), saved_preacts[0, 0], norm_gain, gate_weight[0], up_weight[0],
        down_weight[0])
    return outputs[None], grads[None]


def solution(mesh):
    tokens = P("pipe", "ep", None)
    in_specs = (tokens,) * 7 + (P("pipe", "ep", None, None), P("pipe", None), P("pipe", None, "ep"),
                                P("pipe", None, "ep"), tokens)
    return jax.shard_map(on_device, mesh=mesh, in_specs=in_specs, out_specs=(tokens, tokens), check_vma=False)
```

time: 208 us -> 178 us (0.86); the launches traced: 204 us -> 178 us
  Pallas kernels: 195 us -> 174 us
  local copies, waits for them, and re-layouts: 8.69 us -> 3.17 us
    pallas_call x1, Pallas kernels: 195 us -> 174 us  [on_device(): call(forward_inputs[0], backward_cotangent[0], backward_inputs[0], row(fo...]
    squeeze x4 -> x0, local copies, waits for them, and re-layouts: 5.53 us -> none  [the longest x1 1.39 us: on_device(): forward_routes[0]]
where the time goes in v2:
time: 178 us
  Pallas kernels  174 us (98%)
  local copies, waits for them, and re-layouts  3.17 us (2%)
    pallas_call x1, Pallas kernels, on_device(): call(forward_inputs[0], backward_cotangent[0], backward_inputs[0], row(fo...  174 us

profile of v2, /device:TPU:1, one launch (start us, length us, event | category | flops | bytes accessed | tf_op | source)
XLA Modules:
  0.0 178.3 jit_solution(7264533733984889866)
XLA Ops:
  0.6 174.5 %shard_map.131 = (bf16[128,3584]{1,0:T(8,128)(2,1)}, bf16[128,3584]{1,0:T(8,128)(2,1)}) custom-call(bf16[128,3584]{1,0:T(8,128)(2,1)} %bitcast.18, bf16[128,3584]{1,0:T(8,128)(2,1)} %bitcast.19, bf16[128,3584]{1,0:T(8,128)(2,1)} %bitcast.20, s32[1,128]{1,0:T(1,128)} %bitcast.22, f32[1,128]{1,0:T(1,128)} %bitcast.23, s32[1,128]{1,0:T(1,128)} %bitcast.24, ...), custom_call_target="tpu_custom_call" | custom-call | flops 10000000000 | bytes 20000000 | tf_op jit(solution)/shard_map/pallas_call | solution.py:509
  175.1 0.0 copy-start
  175.1 2.2 %copy.16 = bf16[1,128,3584]{2,1,0:T(8,128)(2,1)} copy(bf16[1,128,3584]{2,1,0:T(8,128)(2,1)} %bitcast.14) | data formatting | bytes 1835008
  177.3 0.0 copy-done
  177.3 0.9 copy.17
Async XLA Ops:
  175.1 2.3 %copy-start = (bf16[128,3584]{1,0:T(8,128)(2,1)S(1)}, bf16[128,3584]{1,0:T(8,128)(2,1)}, u32[]{:S(2)}) copy-start(bf16[128,3584]{1,0:T(8,128)(2,1)} %get-tuple-element.5) | copy-start | bytes 2752516

commit v3 on v2

--- a/solution.py
+++ b/solution.py
@@ -62,7 +62,7 @@
            arr, ret, kept, saved, wg, wu, wd, put, get_m, pack_m, unpack_m, normed, send, recv, xs, xb, hs, hf, gs,
            ghb, factor, gj, tsend, tnear, tfin, rs_in, rs_left, rs_right, ys, gnorm,
            loc_sem, p_send, p_recv, w_send, w_recv, d_send, d_recv, a_send, a_recv, h_send, h_recv, g_send, g_recv,
-           r_send, r_recv):
+           r_send, r_recv, b_send, b_recv):
     p, ep = lax.axis_index("pipe"), lax.axis_index("ep")
     e, k = ep // RING, ep % RING
     right = (p, e * RING + (k + 1) % RING)
@@ -242,11 +242,10 @@
         return x_f, x_g
 
     def weights_on(part):
-        size = HID // 4
-        a, b = pl.ds(part * size, size), pl.ds(HID // 2 + part * size, size)
+        cols = pl.ds(part * 2 * HALF, 2 * HALF)
         o = 4 + 2 * part
-        return (remote(wd.at[3, a], wd.at[2, a], w_send.at[o], w_recv.at[o], right),
-                remote(wd.at[1, b], wd.at[2, b], w_send.at[o + 1], w_recv.at[o + 1], left))
+        return (remote(wd.at[3, HA, cols], wd.at[2, HA, cols], w_send.at[o], w_recv.at[o], right),
+                remote(wd.at[1, HB, cols], wd.at[2, HB, cols], w_send.at[o + 1], w_recv.at[o + 1], left))
 
     def grad_hidden(r):
         return nt(xb[...], wd[r]).astype(BF16)
@@ -309,37 +308,48 @@
         gj[r, :, :HID] = (grad * factor[r, :, :HID]).astype(BF16)
         gj[r, :, HID:] = (grad * factor[r, :, HID:]).astype(BF16)
 
-    def partial(r, q):
+    def partial(r, q, rows):
         cols = pl.ds(q * HALF, HALF)
-        return nt(gj[r, :, :HID], wg[cols, :]) + nt(gj[r, :, HID:], wu[cols, :])
+        return nt(gj[r, rows, :HID], wg[cols, :]) + nt(gj[r, rows, HID:], wu[cols, :])
 
     quarters = [pl.ds(q * HALF, HALF) for q in range(2 * NCH)]
-    near = [1 if q % 2 == 0 else 3 for q in range(2 * NCH)]
-    arrived = {1: rs_left, 3: rs_right}
+    cut = [64, 80, 64, 80]
+    upper = [pl.ds(0, n) for n in cut]
+    lower = [pl.ds(n, ROWS - n) for n in cut]
+
+    def ring_copy(i, q, kind, rows, target, device):
+        cols = quarters[q]
+        n = 6 * q + 2 * kind + i
+        return remote(tsend.at[kind, rows, cols], target.at[rows, cols], r_send.at[n], r_recv.at[n], device)
 
     def send_single(q):
-        cols, far = quarters[q], 4 - near[q]
-        tsend[1, :, cols] = partial(far, q).astype(BF16)
-        return remote(tsend.at[1, :, cols], arrived[far].at[:, cols], r_send.at[3 * q], r_recv.at[3 * q], ring[far])
+        cols, a, b = quarters[q], upper[q], lower[q]
+        tsend[1, a, cols] = partial(3, q, a).astype(BF16)
+        one = ring_copy(0, q, 1, a, rs_right, left)
+        tsend[1, b, cols] = partial(1, q, b).astype(BF16)
+        return one, ring_copy(1, q, 1, b, rs_left, right)
 
     def send_first(q):
-        cols = quarters[q]
-        tsend[0, :, cols] = partial(2, q).astype(BF16)
-        return remote(tsend.at[0, :, cols], rs_in.at[:, cols], r_send.at[3 * q + 1], r_recv.at[3 * q + 1],
-                      ring[near[q]])
+        cols, a, b = quarters[q], upper[q], lower[q]
+        tsend[0, :, cols] = partial(2, q, pl.ds(0, ROWS)).astype(BF16)
+        return ring_copy(0, q, 0, a, rs_in, right), ring_copy(1, q, 0, b, rs_in, left)
 
     def own_parts(q):
-        cols = quarters[q]
-        tnear[:, cols] = partial(near[q], q)
-        tfin[:, cols] = partial(0, q)
+        cols, a, b = quarters[q], upper[q], lower[q]
+        tnear[a, cols] = partial(1, q, a)
+        tnear[b, cols] = partial(3, q, b)
+        tfin[:, cols] = partial(0, q, pl.ds(0, ROWS))
 
     def send_sum(q, first):
-        cols = quarters[q]
+        cols, a, b = quarters[q], upper[q], lower[q]
         with jax.named_scope(f"rs first wait {q}"):
-            first.wait_recv()
-        tsend[2, :, cols] = (tnear[:, cols] + rs_in[:, cols].astype(F32)).astype(BF16)
-        return remote(tsend.at[2, :, cols], arrived[near[q]].at[:, cols], r_send.at[3 * q + 2],
-                      r_recv.at[3 * q + 2], ring[near[q]])
+            first[0].wait_recv()
+        tsend[2, a, cols] = (tnear[a, cols] + rs_in[a, cols].astype(F32)).astype(BF16)
+        one = ring_copy(0, q, 2, a, rs_left, right)
+        with jax.named_scope(f"rs first wait {q} b"):
+            first[1].wait_recv()
+        tsend[2, b, cols] = (tnear[b, cols] + rs_in[b, cols].astype(F32)).astype(BF16)
+        return one, ring_copy(1, q, 2, b, rs_right, left)
 
     def give_back(i, c):
         for m in range(4):
@@ -352,26 +362,32 @@
         for j in range(NSUB):
             ys[i, c, j * ROWS:(j + 1) * ROWS, h * 128:(h + 1) * 128] = total[:, j * 128:(j + 1) * 128]
 
-    with jax.named_scope("gh 1 3 wait"):
-        g1.wait_recv()
-        g3.wait_recv()
-    with jax.named_scope("singles 01"):
-        for r in (1, 3, 0):
-            grad_group(r)
-        singles = [send_single(0), send_single(1)]
-    with jax.named_scope("wd on wait"):
-        for pair in w_on:
-            for copy in pair:
-                copy.wait_recv()
-    with jax.named_scope("gh 2"):
-        g2 = give_grad(2)
-    with jax.named_scope("singles 23"):
-        singles += [send_single(2), send_single(3)]
-
-    with jax.named_scope("h wait"):
-        for copy in (h1, h3, h2):
-            copy.wait_recv()
-    for c in range(NCH):
+    def give_back_quarter(q):
+        c, lanes = q // 2, pl.ds(q % 2 * 128, 128)
+        for m in range(4):
+            part = pl.ds(m * 256, 256)
+            send[3, c, part, lanes] = nn(pack_m[part, :], ys[1, c, :, lanes]).astype(BF16)
+
+        def one(d, carry):
+            to = (e + d) % NEXP
+            pltpu.make_async_remote_copy(
+                src_ref=send.at[3, c, pl.ds(pl.multiple_of(to * BLK, BLK), BLK), lanes],
+                dst_ref=recv.at[3, c, pl.ds(pl.multiple_of(e * BLK, BLK), BLK), lanes],
+                send_sem=b_send.at[q], recv_sem=b_recv.at[q],
+                device_id=(p, to * RING + k), device_id_type=MESH).start()
+            return carry
+        lax.fori_loop(1, NEXP, one, 0)
+        own = pl.ds(pl.multiple_of(e * BLK, BLK), BLK)
+        recv[3, c, own, lanes] = send[3, c, own, lanes]
+
+    def whole_quarter(q):
+        c, lanes = q // 2, pl.ds(q % 2 * 128, 128)
+        part = pl.ds(0, PACK - BLK)
+        return pltpu.make_async_remote_copy(
+            src_ref=send.at[3, c, part, lanes], dst_ref=recv.at[3, c, part, lanes],
+            send_sem=b_send.at[q], recv_sem=b_recv.at[q], device_id=right, device_id_type=MESH)
+
+    def forward_out(c):
         with jax.named_scope(f"out f {c}"):
             for h in range(2):
                 total = nn(hf[0], wd[0, :, half(c, h)])
@@ -380,65 +396,89 @@
                 stack_up(0, c, h, total)
             give_back(0, c)
 
-    with jax.named_scope("gh 2 wait"):
-        g2.wait_recv()
-    with jax.named_scope("firsts"):
-        grad_group(2)
-        firsts = [send_first(0), send_first(1), send_first(2)]
-        own_parts(0)
-        own_parts(1)
-    summed = [send_sum(0, firsts[0]), send_sum(1, firsts[1])]
-    with jax.named_scope("first 3"):
-        firsts.append(send_first(3))
-        own_parts(2)
-        own_parts(3)
-    summed += [send_sum(2, firsts[2]), send_sum(3, firsts[3])]
+    with jax.named_scope("gh 1 3 wait"):
+        g1.wait_recv()
+        g3.wait_recv()
+    with jax.named_scope("singles 0"):
+        for r in (1, 3, 0):
+            grad_group(r)
+        singles = [send_single(0)]
+    with jax.named_scope("h wait"):
+        for copy in (h1, h3, h2):
+            copy.wait_recv()
+    with jax.named_scope("wd on wait 0"):
+        for copy in w_on[0]:
+            copy.wait_recv()
+    forward_out(0)
+    singles.append(send_single(1))
+    with jax.named_scope("wd on wait 1"):
+        for copy in w_on[1]:
+            copy.wait_recv()
+    with jax.named_scope("gh 2"):
+        g2 = give_grad(2)
+    with jax.named_scope("singles 23"):
+        singles += [send_single(2), send_single(3)]
+    forward_out(1)
 
     gate_f = as_column(gates_f[...].astype(BF16).astype(F32))
     gate_b = as_column(gates_b[...].astype(BF16).astype(F32))
-
-    def home(i, c, use):
-        def one(j, carry):
-            got = nn(get_m[i, pl.ds(pl.multiple_of(j * TOK, TOK), TOK), :], recv[2 + i, c])
-            use(col(c, 0, j), got[:, :128])
-            use(col(c, 1, j), got[:, 128:])
-            return carry
-        lax.fori_loop(0, NSUB, one, 0)
-
-    def add_forward(cols, got):
-        out_f[:, cols] = (arr[:, cols].astype(F32) + gate_f * got).astype(BF16)
+    kept_wide = kept[...].astype(F32)
+    inverse_b = lax.rsqrt(jnp.mean(kept_wide * kept_wide, axis=-1, keepdims=True) + EPS)
 
     def home_forward(c):
         with jax.named_scope(f"home f wait {c}"):
             whole(2, c).wait_recv()
-        home(0, c, add_forward)
-
-    def finish_sums(c):
-        for h in range(2):
-            q = 2 * c + h
-            cols = quarters[q]
-            with jax.named_scope(f"rs final wait {q}"):
-                singles[q].wait_recv()
-                summed[q].wait_recv()
-            stack_up(1, c, h, tfin[:, cols] + rs_left[:, cols].astype(F32) + rs_right[:, cols].astype(F32))
-        with jax.named_scope(f"give back b {c}"):
-            give_back(1, c)
-
-    kept_wide = kept[...].astype(F32)
-    inverse_b = lax.rsqrt(jnp.mean(kept_wide * kept_wide, axis=-1, keepdims=True) + EPS)
-
-    def keep(cols, got):
-        gnorm[:, cols] = gate_b * got * gain_ref[:, cols]
-
-    home_forward(0)
-    finish_sums(0)
-    home_forward(1)
-    finish_sums(1)
-
-    for c in range(NCH):
-        with jax.named_scope(f"home b wait {c}"):
-            whole(3, c).wait_recv()
-        home(1, c, keep)
+
+        def one(j, carry):
+            got = nn(get_m[0, pl.ds(pl.multiple_of(j * TOK, TOK), TOK), :], recv[2, c])
+            for h in range(2):
+                cols = col(c, h, j)
+                out_f[:, cols] = (arr[:, cols].astype(F32) + gate_f * got[:, h * 128:(h + 1) * 128]).astype(BF16)
+            return carry
+        lax.fori_loop(0, NSUB, one, 0)
+
+    def home_backward(q):
+        with jax.named_scope(f"home b wait {q}"):
+            whole_quarter(q).wait_recv()
+        c, h = q // 2, q % 2
+
+        def one(j, carry):
+            got = nn(get_m[1, pl.ds(pl.multiple_of(j * TOK, TOK), TOK), :], recv[3, c, :, h * 128:(h + 1) * 128])
+            cols = col(c, h, j)
+            gnorm[:, cols] = gate_b * got * gain_ref[:, cols]
+            return carry
+        lax.fori_loop(0, NSUB, one, 0)
+
+    def finish_sum(q):
+        cols = quarters[q]
+        with jax.named_scope(f"rs final wait {q}"):
+            for copy in singles[q] + summed[q]:
+                copy.wait_recv()
+        stack_up(1, q // 2, q % 2, tfin[:, cols] + rs_left[:, cols].astype(F32) + rs_right[:, cols].astype(F32))
+        with jax.named_scope(f"give back b {q}"):
+            give_back_quarter(q)
+
+    with jax.named_scope("gh 2 wait"):
+        g2.wait_recv()
+    summed = []
+    with jax.named_scope("firsts"):
+        grad_group(2)
+        firsts = [send_first(0), send_first(1)]
+        own_parts(0)
+        own_parts(1)
+    for q in range(2 * NCH):
+        summed.append(send_sum(q, firsts[q]))
+        if q + 2 < 2 * NCH:
+            firsts.append(send_first(q + 2))
+            own_parts(q + 2)
+        if q > 0:
+            finish_sum(q - 1)
+        if q > 1:
+            home_forward(q - 2)
+    finish_sum(2 * NCH - 1)
+
+    for q in range(2 * NCH):
+        home_backward(q)
     with jax.named_scope("final"):
         scaled = gnorm[...]
         xhat = kept[...].astype(F32) * inverse_b
@@ -447,9 +487,11 @@
 
     for copy in pending:
         copy.wait_send()
-    for i in range(4):
+    for i in range(3):
         for c in range(NCH):
             whole(i, c).wait_send()
+    for q in range(2 * NCH):
+        whole_quarter(q).wait_send()
 
 
 def on_device(forward_inputs, forward_routes, forward_gates, backward_inputs, backward_cotangent, backward_routes,
@@ -490,7 +532,7 @@
         pltpu.VMEM((2, NCH, NSUB * ROWS, 256), BF16),
         pltpu.VMEM((TOK, D), F32),
         dma((5,)), dma((2,)), dma((2,)), dma((8,)), dma((8,)), dma((8,)), dma((8,)), dma((12,)), dma((12,)),
-        dma((3,)), dma((3,)), dma((3,)), dma((3,)), dma((12,)), dma((12,)),
+        dma((3,)), dma((3,)), dma((3,)), dma((3,)), dma((24,)), dma((24,)), dma((4,)), dma((4,)),
     ]
     call = pl.pallas_call(
         kernel,

time: 178 us -> 167 us (0.938)
  Pallas kernels: 174 us -> 163 us
    pallas_call x1, Pallas kernels: 174 us -> 163 us  [on_device(): call(forward_inputs[0], backward_cotangent[0], backward_inputs[0], row(fo...]
where the time goes in v3:
time: 167 us
  Pallas kernels  163 us (98%)
  local copies, waits for them, and re-layouts  3.17 us (2%)
    pallas_call x1, Pallas kernels, on_device(): call(forward_inputs[0], backward_cotangent[0], backward_inputs[0], row(fo...  163 us

profile of v3, /device:TPU:1, one launch (start us, length us, event | category | flops | bytes accessed | tf_op | source)
XLA Modules:
  0.0 167.2 jit_solution(2723691444350904554)
XLA Ops:
  0.6 163.4 %shard_map.131 = (bf16[128,3584]{1,0:T(8,128)(2,1)}, bf16[128,3584]{1,0:T(8,128)(2,1)}) custom-call(bf16[128,3584]{1,0:T(8,128)(2,1)} %bitcast.18, bf16[128,3584]{1,0:T(8,128)(2,1)} %bitcast.19, bf16[128,3584]{1,0:T(8,128)(2,1)} %bitcast.20, s32[1,128]{1,0:T(1,128)} %bitcast.22, f32[1,128]{1,0:T(1,128)} %bitcast.23, s32[1,128]{1,0:T(1,128)} %bitcast.24, ...), custom_call_target="tpu_custom_call" | custom-call | flops 10000000000 | bytes 20000000 | tf_op jit(solution)/shard_map/pallas_call | solution.py:551
  164.0 0.0 copy-start
  164.0 2.2 %copy.16 = bf16[1,128,3584]{2,1,0:T(8,128)(2,1)} copy(bf16[1,128,3584]{2,1,0:T(8,128)(2,1)} %bitcast.14) | data formatting | bytes 1835008
  166.3 0.0 copy-done
  166.3 0.9 copy.17
Async XLA Ops:
  164.0 2.3 %copy-start = (bf16[128,3584]{1,0:T(8,128)(2,1)S(1)}, bf16[128,3584]{1,0:T(8,128)(2,1)}, u32[]{:S(2)}) copy-start(bf16[128,3584]{1,0:T(8,128)(2,1)} %get-tuple-element.5) | copy-start | bytes 2752516

commit v4 on v3

v4 whole, which is shorter than its diff:
```python
import functools
import jax
import jax.numpy as jnp
from jax import lax
from jax.experimental import pallas as pl
from jax.experimental.pallas import tpu as pltpu
from jax.sharding import PartitionSpec as P


RING = 4
NEXP = 16
TOK = 128
D = 3584
HID = 256
CAP = 9
ROWS = NEXP * CAP
NCH = 2
NSUB = 7
HALF = NSUB * 128
BLK = 64
PACK = NEXP * BLK
EPS = 1e-6
MESH = pl.DeviceIdType.MESH
F32 = jnp.float32
BF16 = jnp.bfloat16


def iota(shape, dim):
    return lax.broadcasted_iota(jnp.int32, shape, dim)


def nn(a, b):
    return lax.dot_general(a, b, (((1,), (0,)), ((), ())), preferred_element_type=F32)


def nt(a, b):
    return lax.dot_general(a, b, (((1,), (1,)), ((), ())), preferred_element_type=F32)


def hot(mask):
    return jnp.where(mask, 1.0, 0.0).astype(BF16)


def as_column(row):
    t0, t1 = iota((TOK, TOK), 0), iota((TOK, TOK), 1)
    return jnp.sum(jnp.where(t0 == t1, jnp.broadcast_to(row, (TOK, TOK)), 0.0), axis=1, keepdims=True)


def slot_places(routes):
    t0, t1 = iota((TOK, TOK), 0), iota((TOK, TOK), 1)
    row = routes.astype(F32)
    column = as_column(row)
    same = column == row
    col_before = jnp.sum(jnp.where(same & (t1 < t0), 1.0, 0.0), axis=1, keepdims=True)
    row_before = jnp.sum(jnp.where(same & (t0 < t1), 1.0, 0.0), axis=0, keepdims=True)
    col = column * BLK + col_before
    return (row * BLK + row_before).astype(jnp.int32), col.astype(jnp.int32)


def kernel(fin, cot, bin_hbm, routes_f, gates_f, routes_b, gates_b, saved_hbm, gain_ref, wg_hbm, wu_hbm, wd_hbm,
           out_f, out_b,
           arr, ret, kept, saved, wg, wu, wd, put, get_m, pack_m, unpack_m, next_routes, next_gain, normed, send, recv, xs, xb, xbn, hk, hs, hp,
           hn, fs, fr, gsn, gpn, gsp, ghb, factor, gj, tsend, tnear, tfin, rs_in, rs_p, rs_n, ys, gnorm,
           loc_sem, p_send, p_recv, w_send, w_recv, d_send, d_recv, a_send, a_recv, h_send, h_recv, g_send, g_recv,
           r_send, r_recv, b_send, b_recv):
    p, ep = lax.axis_index("pipe"), lax.axis_index("ep")
    e, k = ep // RING, ep % RING
    groups = (k, k + 1 - 2 * (k % 2), RING - 1 - k, (k + 2) % RING)
    pair, next_pair = (p, e * RING + groups[1]), (p, e * RING + groups[2])
    after, before = ((p + 1) % 4, ep), ((p + 3) % 4, ep)
    pending = []

    def remote(src, dst, ssem, rsem, device):
        copy = pltpu.make_async_remote_copy(src_ref=src, dst_ref=dst, send_sem=ssem, recv_sem=rsem, device_id=device,
                                            device_id_type=MESH)
        copy.start()
        pending.append(copy)
        return copy

    loads = [pltpu.make_async_copy(a, b, loc_sem.at[i]) for i, (a, b) in enumerate(
        ((fin, normed), (wd_hbm, wd.at[0]), (wg_hbm, wg), (wu_hbm, wu), (saved_hbm, saved), (bin_hbm, kept)))]
    for load in loads:
        load.start()

    barrier = pltpu.get_barrier_semaphore()

    def greet(d, carry):
        pl.semaphore_signal(barrier, inc=1, device_id=(p, (e + d) % NEXP * RING + k), device_id_type=MESH)
        return carry

    def greet_before(d, carry):
        pl.semaphore_signal(barrier, inc=1, device_id=((p + 3) % 4, (e + d) % NEXP * RING + k), device_id_type=MESH)
        return carry

    lax.fori_loop(1, NEXP, greet, 0)
    lax.fori_loop(0, NEXP, greet_before, 0)
    for device in (pair, next_pair, after):
        pl.semaphore_signal(barrier, inc=1, device_id=device, device_id_type=MESH)
    with jax.named_scope("barrier wait"):
        pl.semaphore_wait(barrier, NEXP - 1 + NEXP + 3)

    to_routes = remote(routes_f, next_routes, p_send.at[2], p_recv.at[2], before)
    to_gain = remote(gain_ref, next_gain, p_send.at[3], p_recv.at[3], before)
    pipe_b = remote(cot, ret, p_send.at[1], p_recv.at[1], before)
    HA, HB = pl.ds(0, HID // 2), pl.ds(HID // 2, HID // 2)
    F1, F2 = pl.ds(0, 2 * HALF), pl.ds(2 * HALF, 2 * HALF)
    w_pb = remote(wd_hbm.at[HB, F1], wd.at[1, HB, F1], w_send.at[0], w_recv.at[0], pair)
    w_na = remote(wd_hbm.at[HA, F1], wd.at[2, HA, F1], w_send.at[1], w_recv.at[1], next_pair)
    w_pa = remote(wd_hbm.at[HA, F1], wd.at[1, HA, F1], w_send.at[2], w_recv.at[2], pair)
    w_nb = remote(wd_hbm.at[HB, F1], wd.at[2, HB, F1], w_send.at[3], w_recv.at[3], next_pair)

    def put_matrix(i, places):
        def one(j, carry):
            put[i, :, pl.ds(pl.multiple_of(j * 128, 128), 128)] = hot(iota((PACK, TOK), 0) == places + j * CAP)
            return carry
        lax.fori_loop(0, NSUB, one, 0)

    def get_matrix(i, places):
        def one(j, carry):
            get_m[i, pl.ds(pl.multiple_of(j * 128, 128), 128), :] = hot(iota((TOK, PACK), 1) == places + j * CAP)
            return carry
        lax.fori_loop(0, NSUB, one, 0)

    def ninth(v):
        return (v * 57) >> 9

    def unpack_matrix():
        def one(j, carry):
            r = iota((ROWS, PACK), 0)
            unpack_m[pl.ds(pl.multiple_of(j * ROWS, 16), ROWS), :] = hot(
                iota((ROWS, PACK), 1) == ninth(r) * (BLK - CAP) + r + j * CAP)
            return carry
        lax.fori_loop(0, NSUB, one, 0)

    def pack_matrix():
        for j in range(NSUB):
            r = iota((PACK, ROWS), 1)
            pack_m[:, j * ROWS:(j + 1) * ROWS] = hot(
                iota((PACK, ROWS), 0) == ninth(r) * (BLK - CAP) + r + j * CAP)

    def place(d):
        odd = d % 2
        return (e + odd * ((d + 1) // 2) + (1 - odd) * (NEXP - d // 2)) % NEXP

    def spread(i, c):
        s = 2 * i + c
        section = (p + 1) % 4 if i == 0 else p

        own = pl.ds(pl.multiple_of(e * BLK, BLK), BLK)

        def block(to):
            pltpu.make_async_remote_copy(
                src_ref=send.at[i, c, pl.ds(pl.multiple_of(to * BLK, BLK), BLK)], dst_ref=recv.at[i, c, own],
                send_sem=d_send.at[s], recv_sem=d_recv.at[s],
                device_id=(section, to * RING + k), device_id_type=MESH).start()

        def one(d, carry):
            block(place(d))
            return carry
        lax.fori_loop(1, NEXP, one, 0)
        if i > 0:
            recv[i, c, own, :] = send[i, c, own, :]
        else:
            block(e)

    def whole(i, c):
        part = pl.ds(0, PACK if i == 0 else PACK - BLK)
        return pltpu.make_async_remote_copy(
            src_ref=send.at[i, c, part], dst_ref=recv.at[i, c, part],
            send_sem=d_send.at[2 * i + c], recv_sem=d_recv.at[2 * i + c], device_id=pair, device_id_type=MESH)

    def half(c, h):
        return pl.ds((2 * c + h) * HALF, HALF)

    def col(c, h, j):
        return pl.ds(pl.multiple_of((2 * c + h) * HALF + j * 128, 128), 128)

    def dispatch(i, values, order):
        for c in order:
            stack = jnp.concatenate([
                jnp.concatenate([values[:, (2 * c + h) * HALF + j * 128:(2 * c + h) * HALF + (j + 1) * 128]
                                 for h in range(2)], axis=1) for j in range(NSUB)], axis=0)
            for m in range(4):
                part = pl.ds(m * 256, 256)
                send[i, c, part, :] = nn(put[i, part, :], stack).astype(BF16)
            spread(i, c)

    def unpack(i, c, target):
        def one(j, carry):
            got = nn(unpack_m[pl.ds(pl.multiple_of(j * ROWS, 16), ROWS), :], recv[i, c]).astype(BF16)
            target[:, col(c, 0, j)] = got[:, :128]
            target[:, col(c, 1, j)] = got[:, 128:]
            return carry
        lax.fori_loop(0, NSUB, one, 0)

    def saved_factors(r):
        group = groups[r]
        q = iota((ROWS, NEXP * RING * CAP), 0)
        take = hot(iota((ROWS, NEXP * RING * CAP), 1) == ninth(q) * (RING - 1) * CAP + q + group * CAP)
        pre = nn(take, saved[...])
        gate, up = pre[:, :HID], pre[:, HID:]
        sigma = 1.0 / (1.0 + jnp.exp(-gate))
        factor[r, :, :HID] = up * sigma * (1.0 + gate * (1.0 - sigma))
        factor[r, :, HID:] = gate * sigma

    loads[0].wait()
    wide = normed[...].astype(F32)
    inverse = lax.rsqrt(jnp.mean(wide * wide, axis=-1, keepdims=True) + EPS)
    with jax.named_scope("routes wait"):
        to_routes.wait_recv()
        to_gain.wait_recv()
    put_matrix(0, slot_places(next_routes[...])[0])
    normed[...] = (wide * inverse * next_gain[...]).astype(BF16)
    with jax.named_scope("dispatch f"):
        dispatch(0, normed, (0, 1))

    cols_f = slot_places(routes_f[...])[1]
    rows_b, cols_b = slot_places(routes_b[...])
    put_matrix(1, rows_b)
    unpack_matrix()
    for load in loads[1:]:
        load.wait()
    with jax.named_scope("saved factors"):
        for r in range(RING):
            saved_factors(r)

    with jax.named_scope("wd fwd wait"):
        w_na.wait_recv()
    w_pf = remote(wd.at[2, HA, F1], wd.at[3, HA, F1], w_send.at[4], w_recv.at[4], pair)
    w_pb.wait_recv()
    w_nf = remote(wd.at[1, HB, F1], wd.at[3, HB, F1], w_send.at[5], w_recv.at[5], next_pair)

    def gather(c):
        with jax.named_scope(f"f disp wait {c}"):
            whole(0, c).wait_recv()
        unpack(0, c, xs.at[0])
        A, B = half(c, 0), half(c, 1)
        o = 6 * c
        x_pb = remote(xs.at[0, :, B], xs.at[1, :, B], a_send.at[o], a_recv.at[o], pair)
        x_na = remote(xs.at[0, :, A], xs.at[2, :, A], a_send.at[o + 1], a_recv.at[o + 1], next_pair)
        x_pa = remote(xs.at[0, :, A], xs.at[1, :, A], a_send.at[o + 2], a_recv.at[o + 2], pair)
        x_nb = remote(xs.at[0, :, B], xs.at[2, :, B], a_send.at[o + 3], a_recv.at[o + 3], next_pair)
        return x_pb, x_na, x_pa, x_nb

    def on_to_pair(c):
        A, o = half(c, 0), 6 * c + 4
        return remote(xs.at[2, :, A], xs.at[3, :, A], a_send.at[o], a_recv.at[o], pair)

    def on_to_next(c):
        B, o = half(c, 1), 6 * c + 5
        return remote(xs.at[1, :, B], xs.at[3, :, B], a_send.at[o], a_recv.at[o], next_pair)

    def hidden(r):
        rows = xs[r]
        pre_gate = nn(rows, wg[...])
        pre_up = nn(rows, wu[...])
        return (pre_gate / (1.0 + jnp.exp(-pre_gate)) * pre_up).astype(BF16)

    gathers = [gather(0)]

    with jax.named_scope("pipe b wait"):
        pipe_b.wait_recv()
    with jax.named_scope("dispatch b"):
        dispatch(1, ret, (1, 0))
    pipe_f = remote(fin, arr, p_send.at[0], p_recv.at[0], after)

    gathers.append(gather(1))
    with jax.named_scope("hidden 0"):
        hk[0] = hidden(0)

    with jax.named_scope("matrices"):
        pack_matrix()
        get_matrix(0, cols_f)
        get_matrix(1, cols_b)

    x_on = []
    for c in range(NCH):
        with jax.named_scope(f"x na pb wait {c}"):
            gathers[c][1].wait_recv()
            x_on.append(on_to_pair(c))
            gathers[c][0].wait_recv()
            x_on.append(on_to_next(c))

    def exchange_f2(i, rows):
        cols = (rows, F2)
        return remote(wd_hbm.at[cols], wd.at[(1,) + cols], w_send.at[6 + i], w_recv.at[6 + i], pair)

    with jax.named_scope("b disp wait 1"):
        whole(1, 1).wait_recv()
    unpack(1, 1, xb)
    b_rows = remote(xb.at[:, F2], xbn, g_send.at[0], g_recv.at[0], next_pair)
    w_f2 = [exchange_f2(0, HA)]
    with jax.named_scope("b disp wait 0"):
        whole(1, 0).wait_recv()
    unpack(1, 0, xb)
    with jax.named_scope("wd F1 wait"):
        for copy in (w_pa, w_nb, w_pf, w_nf):
            copy.wait_recv()
    with jax.named_scope("gh F1"):
        for r in (2, 3):
            gsn[:, (r - 2) * HID:(r - 1) * HID] = nt(xb[:, F1], wd[r, :, F1]).astype(BF16)
        b_part = remote(gsn, gpn, g_send.at[1], g_recv.at[1], next_pair)
        ghb[0] = nt(xb[...], wd[0]).astype(BF16)

    with jax.named_scope("x rest wait"):
        for c in range(NCH):
            gathers[c][2].wait_recv()
            gathers[c][3].wait_recv()
    with jax.named_scope("hidden 2 1"):
        hk[1] = hidden(2)
        h_n0 = remote(hk.at[1], hn.at[0], h_send.at[0], h_recv.at[0], next_pair)
        hs[0] = hidden(1)
        h_p0 = remote(hs.at[0], hp.at[0], h_send.at[1], h_recv.at[1], pair)
    with jax.named_scope("x on wait"):
        for copy in x_on:
            copy.wait_recv()
    with jax.named_scope("hidden 3"):
        hs[1] = hidden(3)
        h_p1 = remote(hs.at[1], hp.at[1], h_send.at[2], h_recv.at[2], pair)
    w_f2.append(exchange_f2(1, HB))

    def grad_group(r):
        grad = ghb[r].astype(F32)
        gj[r, :, :HID] = (grad * factor[r, :, :HID]).astype(BF16)
        gj[r, :, HID:] = (grad * factor[r, :, HID:]).astype(BF16)

    def partial(r, q, rows):
        cols = pl.ds(q * HALF, HALF)
        return nt(gj[r, rows, :HID], wg[cols, :]) + nt(gj[r, rows, HID:], wu[cols, :])

    quarters = [pl.ds(q * HALF, HALF) for q in range(2 * NCH)]
    cut = [80, 64, 80, 64]
    upper = [pl.ds(0, n) for n in cut]
    lower = [pl.ds(n, ROWS - n) for n in cut]

    def ring_copy(i, q, kind, rows, target, device):
        cols = quarters[q]
        n = 6 * q + 2 * kind + i
        return remote(tsend.at[kind, rows, cols], target.at[rows, cols], r_send.at[n], r_recv.at[n], device)

    def send_single_pair(q):
        cols, a = quarters[q], upper[q]
        tsend[1, a, cols] = partial(1, q, a).astype(BF16)
        return ring_copy(0, q, 1, a, rs_p, pair)

    def send_single_next(q):
        cols, b = quarters[q], lower[q]
        tsend[1, b, cols] = partial(2, q, b).astype(BF16)
        return ring_copy(1, q, 1, b, rs_n, next_pair)

    def send_first(q):
        cols, a, b = quarters[q], upper[q], lower[q]
        tsend[0, :, cols] = partial(3, q, pl.ds(0, ROWS)).astype(BF16)
        return ring_copy(0, q, 0, a, rs_in, pair), ring_copy(1, q, 0, b, rs_in, next_pair)

    def own_parts(q):
        cols, a, b = quarters[q], upper[q], lower[q]
        tnear[a, cols] = partial(2, q, a)
        tnear[b, cols] = partial(1, q, b)
        tfin[:, cols] = partial(0, q, pl.ds(0, ROWS))

    def send_sum(q, first):
        cols, a, b = quarters[q], upper[q], lower[q]
        with jax.named_scope(f"rs first wait {q}"):
            first[0].wait_recv()
        tsend[2, a, cols] = (tnear[a, cols] + rs_in[a, cols].astype(F32)).astype(BF16)
        one = ring_copy(0, q, 2, a, rs_n, next_pair)
        with jax.named_scope(f"rs first wait {q} b"):
            first[1].wait_recv()
        tsend[2, b, cols] = (tnear[b, cols] + rs_in[b, cols].astype(F32)).astype(BF16)
        return one, ring_copy(1, q, 2, b, rs_p, pair)

    def give_back(i, c):
        for m in range(4):
            part = pl.ds(m * 256, 256)
            send[2 + i, c, part, :] = nn(pack_m[part, :], ys[i, c]).astype(BF16)
        spread(2 + i, c)

    def stack_up(i, c, h, total):
        total = total.astype(BF16)
        for j in range(NSUB):
            ys[i, c, j * ROWS:(j + 1) * ROWS, h * 128:(h + 1) * 128] = total[:, j * 128:(j + 1) * 128]

    def give_back_quarter(q):
        c, lanes = q // 2, pl.ds(q % 2 * 128, 128)
        send[3, c, :, lanes] = nn(pack_m[...], ys[1, c, :, lanes]).astype(BF16)

        def one(d, carry):
            to = place(d)
            pltpu.make_async_remote_copy(
                src_ref=send.at[3, c, pl.ds(pl.multiple_of(to * BLK, BLK), BLK), lanes],
                dst_ref=recv.at[3, c, pl.ds(pl.multiple_of(e * BLK, BLK), BLK), lanes],
                send_sem=b_send.at[q], recv_sem=b_recv.at[q],
                device_id=(p, to * RING + k), device_id_type=MESH).start()
            return carry
        lax.fori_loop(1, NEXP, one, 0)
        own = pl.ds(pl.multiple_of(e * BLK, BLK), BLK)
        recv[3, c, own, lanes] = send[3, c, own, lanes]

    def whole_quarter(q):
        c, lanes = q // 2, pl.ds(q % 2 * 128, 128)
        part = pl.ds(0, PACK - BLK)
        return pltpu.make_async_remote_copy(
            src_ref=send.at[3, c, part, lanes], dst_ref=recv.at[3, c, part, lanes],
            send_sem=b_send.at[q], recv_sem=b_recv.at[q], device_id=pair, device_id_type=MESH)

    def pair_total(i, cols):
        return nn(hk[i], wd[0, :, cols]) + nn(hp[i], wd[1, :, cols])

    gate_f = as_column(gates_f[...].astype(BF16).astype(F32))
    gate_b = as_column(gates_b[...].astype(BF16).astype(F32))
    kept_wide = kept[...].astype(F32)
    inverse_b = lax.rsqrt(jnp.mean(kept_wide * kept_wide, axis=-1, keepdims=True) + EPS)

    def home_forward(c):
        with jax.named_scope(f"home f wait {c}"):
            if c == 0:
                pipe_f.wait_recv()
            whole(2, c).wait_recv()

        def one(j, carry):
            got = nn(get_m[0, pl.ds(pl.multiple_of(j * TOK, TOK), TOK), :], recv[2, c])
            for h in range(2):
                cols = col(c, h, j)
                out_f[:, cols] = (arr[:, cols].astype(F32) + gate_f * got[:, h * 128:(h + 1) * 128]).astype(BF16)
            return carry
        lax.fori_loop(0, NSUB, one, 0)

    def home_backward(q):
        with jax.named_scope(f"home b wait {q}"):
            whole_quarter(q).wait_recv()
        c, h = q // 2, q % 2

        got = nn(get_m[1], recv[3, c, :, h * 128:(h + 1) * 128])
        inner = jnp.zeros((TOK, 128), F32)
        for j in range(NSUB):
            cols = pl.ds((2 * c + h) * HALF + j * 128, 128)
            scaled = gate_b * got[j * TOK:(j + 1) * TOK] * gain_ref[:, cols]
            gnorm[:, cols] = scaled
            inner = inner + scaled * kept[:, cols].astype(F32)
        return inner

    def finish_sum(q):
        cols = quarters[q]
        with jax.named_scope(f"rs final wait {q}"):
            for copy in (singles_p[q], singles_n[q]) + summed[q]:
                copy.wait_recv()
        stack_up(1, q // 2, q % 2, tfin[:, cols] + rs_p[:, cols].astype(F32) + rs_n[:, cols].astype(F32))
        with jax.named_scope(f"give back b {q}"):
            give_back_quarter(q)

    with jax.named_scope("h pair wait"):
        h_p0.wait_recv()
        h_p1.wait_recv()
    h_n1 = remote(hp.at[1], hn.at[1], h_send.at[3], h_recv.at[3], next_pair)
    grad_group(0)
    with jax.named_scope("b rows wait"):
        b_rows.wait_recv()
        b_part.wait_recv()
    with jax.named_scope("gh 2"):
        ghb[2] = (nt(xbn[...], wd[0, :, F2]) + gpn[:, :HID].astype(F32)).astype(BF16)
        grad_group(2)
    with jax.named_scope("singles next"):
        singles_n = [send_single_next(q) for q in range(2)]
    with jax.named_scope("h next wait"):
        h_n0.wait_recv()
        h_n1.wait_recv()
    with jax.named_scope("out f 0"):
        for h in range(2):
            cols = half(0, h)
            stack_up(0, 0, h, pair_total(0, cols) + nn(hn[0], wd[2, :, cols]) + nn(hn[1], wd[3, :, cols]))
        give_back(0, 0)
    grad_pair = []
    for i, part in enumerate((HA, HB)):
        with jax.named_scope(f"wd F2 wait {i}"):
            w_f2[i].wait_recv()
        with jax.named_scope(f"gh pair {i}"):
            gsp[0, :, part] = nt(xb[...], wd[1, part, :]).astype(BF16)
            grad_pair.append(remote(gsp.at[0, :, part], ghb.at[1, :, part], g_send.at[2 + i], g_recv.at[2 + i], pair))
            other = pl.ds(HID + i * (HID // 2), HID // 2)
            gsp[1, :, part] = (nt(xbn[...], wd[1, part, F2]) + gpn[:, other].astype(F32)).astype(BF16)
            grad_pair.append(remote(gsp.at[1, :, part], ghb.at[3, :, part], g_send.at[4 + i], g_recv.at[4 + i], pair))
    with jax.named_scope("out f part"):
        for h in range(2):
            part = pl.ds(h * HALF, HALF)
            fs[:, part] = pair_total(1, half(1, h)).astype(BF16)
        f_part = remote(fs, fr, h_send.at[4], h_recv.at[4], next_pair)
    with jax.named_scope("gh pair wait"):
        for copy in grad_pair:
            copy.wait_recv()
    singles_p, firsts, summed = [], [], []
    with jax.named_scope("ring sums 0"):
        for r in (1, 3):
            grad_group(r)
        firsts.append(send_first(0))
        singles_p.append(send_single_pair(0))
    with jax.named_scope("ring sums 1"):
        for q in (1, 2):
            firsts.append(send_first(q))
            singles_p.append(send_single_pair(q))
        for q in range(2 * NCH):
            own_parts(q)
    with jax.named_scope("f part wait"):
        f_part.wait_recv()
    with jax.named_scope("out f 1"):
        for h in range(2):
            stack_up(0, 1, h, pair_total(0, half(1, h)) + fr[:, h * HALF:(h + 1) * HALF].astype(F32))
        give_back(0, 1)
    summed.append(send_sum(0, firsts[0]))
    summed.append(send_sum(1, firsts[1]))
    with jax.named_scope("ring sums 3"):
        singles_n.append(send_single_next(2))
        firsts.append(send_first(3))
    summed.append(send_sum(2, firsts[2]))
    with jax.named_scope("ring sums 4"):
        singles_p.append(send_single_pair(3))
        singles_n.append(send_single_next(3))
    finish_sum(0)
    summed.append(send_sum(3, firsts[3]))
    finish_sum(1)
    home_forward(0)
    finish_sum(2)
    home_forward(1)
    finish_sum(3)

    inner = home_backward(0)
    for q in range(1, 2 * NCH):
        inner = inner + home_backward(q)
    with jax.named_scope("final"):
        shift = inverse_b * inverse_b * jnp.sum(inner, axis=-1, keepdims=True) / D
        for q in range(2 * NCH):
            cols = quarters[q]
            out_b[:, cols] = (ret[:, cols].astype(F32) + inverse_b * (
                gnorm[:, cols] - kept[:, cols].astype(F32) * shift)).astype(BF16)

    for copy in pending:
        copy.wait_send()
    for i in range(3):
        for c in range(NCH):
            whole(i, c).wait_send()
    for q in range(2 * NCH):
        whole_quarter(q).wait_send()


def on_device(forward_inputs, forward_routes, forward_gates, backward_inputs, backward_cotangent, backward_routes,
              backward_gates, saved_preacts, norm_gain, gate_weight, up_weight, down_weight):
    vmem = pl.BlockSpec(memory_space=pltpu.VMEM)
    hbm = pl.BlockSpec(memory_space=pl.ANY)
    dma = pltpu.SemaphoreType.DMA
    out = jax.ShapeDtypeStruct((TOK, D), BF16)
    scratch = [
        pltpu.VMEM((TOK, D), BF16),
        pltpu.VMEM((TOK, D), BF16),
        pltpu.VMEM((TOK, D), BF16),
        pltpu.VMEM((RING * ROWS, 2 * HID), BF16),
        pltpu.VMEM((D, HID), BF16),
        pltpu.VMEM((D, HID), BF16),
        pltpu.VMEM((RING, HID, D), BF16),
        pltpu.VMEM((2, PACK, NSUB * TOK), BF16),
        pltpu.VMEM((2, NSUB * TOK, PACK), BF16),
        pltpu.VMEM((PACK, NSUB * ROWS), BF16),
        pltpu.VMEM((NSUB * ROWS, PACK), BF16),
        pltpu.VMEM((1, TOK), jnp.int32),
        pltpu.VMEM((1, D), F32),
        pltpu.VMEM((TOK, D), BF16),
        pltpu.VMEM((4, NCH, PACK, 256), BF16),
        pltpu.VMEM((4, NCH, PACK, 256), BF16),
        pltpu.VMEM((RING, ROWS, D), BF16),
        pltpu.VMEM((ROWS, D), BF16),
        pltpu.VMEM((ROWS, 2 * HALF), BF16),
        pltpu.VMEM((2, ROWS, HID), BF16),
        pltpu.VMEM((2, ROWS, HID), BF16),
        pltpu.VMEM((2, ROWS, HID), BF16),
        pltpu.VMEM((2, ROWS, HID), BF16),
        pltpu.VMEM((ROWS, 2 * HALF), BF16),
        pltpu.VMEM((ROWS, 2 * HALF), BF16),
        pltpu.VMEM((ROWS, 2 * HID), BF16),
        pltpu.VMEM((ROWS, 2 * HID), BF16),
        pltpu.VMEM((2, ROWS, HID), BF16),
        pltpu.VMEM((RING, ROWS, HID), BF16),
        pltpu.VMEM((RING, ROWS, 2 * HID), F32),
        pltpu.VMEM((RING, ROWS, 2 * HID), BF16),
        pltpu.VMEM((3, ROWS, D), BF16),
        pltpu.VMEM((ROWS, D), F32),
        pltpu.VMEM((ROWS, D), F32),
        pltpu.VMEM((ROWS, D), BF16),
        pltpu.VMEM((ROWS, D), BF16),
        pltpu.VMEM((ROWS, D), BF16),
        pltpu.VMEM((2, NCH, NSUB * ROWS, 256), BF16),
        pltpu.VMEM((TOK, D), F32),
        dma((6,)), dma((4,)), dma((4,)), dma((8,)), dma((8,)), dma((8,)), dma((8,)), dma((12,)), dma((12,)),
        dma((5,)), dma((5,)), dma((6,)), dma((6,)), dma((24,)), dma((24,)), dma((4,)), dma((4,)),
    ]
    call = pl.pallas_call(
        kernel,
        out_shape=(out, out),
        in_specs=[hbm, hbm, hbm, vmem, vmem, vmem, vmem, hbm, vmem, hbm, hbm, hbm],
        out_specs=(vmem, vmem),
        scratch_shapes=scratch,
        compiler_params=pltpu.CompilerParams(collective_id=0, has_side_effects=True,
                                             vmem_limit_bytes=62 * 2 ** 20),
        cost_estimate=pl.CostEstimate(flops=10 ** 10, bytes_accessed=2 * 10 ** 7, transcendentals=10 ** 6),
    )

    def row(values):
        return values.reshape(1, TOK)

    outputs, grads = call(
        forward_inputs[0], backward_cotangent[0], backward_inputs[0], row(forward_routes), row(forward_gates),
        row(backward_routes), row(backward_gates), saved_preacts[0, 0], norm_gain, gate_weight[0], up_weight[0],
        down_weight[0])
    return outputs[None], grads[None]


def solution(mesh):
    tokens = P("pipe", "ep", None)
    in_specs = (tokens,) * 7 + (P("pipe", "ep", None, None), P("pipe", None), P("pipe", None, "ep"),
                                P("pipe", None, "ep"), tokens)
    return jax.shard_map(on_device, mesh=mesh, in_specs=in_specs, out_specs=(tokens, tokens), check_vma=False)
```

time: 167 us -> 164 us (0.982)
  Pallas kernels: 163 us -> 160 us
    pallas_call x1, Pallas kernels: 163 us -> 160 us  [on_device(): call(forward_inputs[0], backward_cotangent[0], backward_inputs[0], row(fo...]
where the time goes in v4:
time: 164 us; the launch traced here: 163 us
  Pallas kernels  160 us (98%)
  local copies, waits for them, and re-layouts  3.17 us (2%)
    pallas_call x1, Pallas kernels, on_device(): call(forward_inputs[0], backward_cotangent[0], backward_inputs[0], row(fo...  160 us

profile of v4, /device:TPU:1, one launch (start us, length us, event | category | flops | bytes accessed | tf_op | source)
XLA Modules:
  0.0 163.3 jit_solution(7409842961358436178)
XLA Ops:
  0.6 159.5 %shard_map.131 = (bf16[128,3584]{1,0:T(8,128)(2,1)}, bf16[128,3584]{1,0:T(8,128)(2,1)}) custom-call(bf16[128,3584]{1,0:T(8,128)(2,1)} %bitcast.18, bf16[128,3584]{1,0:T(8,128)(2,1)} %bitcast.19, bf16[128,3584]{1,0:T(8,128)(2,1)} %bitcast.20, s32[1,128]{1,0:T(1,128)} %bitcast.22, f32[1,128]{1,0:T(1,128)} %bitcast.23, s32[1,128]{1,0:T(1,128)} %bitcast.24, ...), custom_call_target="tpu_custom_call" | custom-call | flops 10000000000 | bytes 20000000 | tf_op jit(solution)/shard_map/pallas_call | solution.py:608
  160.2 0.0 copy-start
  160.2 2.2 %copy.16 = bf16[1,128,3584]{2,1,0:T(8,128)(2,1)} copy(bf16[1,128,3584]{2,1,0:T(8,128)(2,1)} %bitcast.14) | data formatting | bytes 1835008
  162.4 0.0 copy-done
  162.4 0.9 copy.17
Async XLA Ops:
  160.2 2.3 %copy-start = (bf16[128,3584]{1,0:T(8,128)(2,1)S(1)}, bf16[128,3584]{1,0:T(8,128)(2,1)}, u32[]{:S(2)}) copy-start(bf16[128,3584]{1,0:T(8,128)(2,1)} %get-tuple-element.5) | copy-start | bytes 2752516

commit v5 on v4

--- a/solution.py
+++ b/solution.py
@@ -329,7 +329,7 @@
         return nt(gj[r, rows, :HID], wg[cols, :]) + nt(gj[r, rows, HID:], wu[cols, :])
 
     quarters = [pl.ds(q * HALF, HALF) for q in range(2 * NCH)]
-    cut = [80, 64, 80, 64]
+    cut = [80, 80, 80, 96]
     upper = [pl.ds(0, n) for n in cut]
     lower = [pl.ds(n, ROWS - n) for n in cut]
 
@@ -348,10 +348,15 @@
         tsend[1, b, cols] = partial(2, q, b).astype(BF16)
         return ring_copy(1, q, 1, b, rs_n, next_pair)
 
-    def send_first(q):
-        cols, a, b = quarters[q], upper[q], lower[q]
-        tsend[0, :, cols] = partial(3, q, pl.ds(0, ROWS)).astype(BF16)
-        return ring_copy(0, q, 0, a, rs_in, pair), ring_copy(1, q, 0, b, rs_in, next_pair)
+    def send_first_pair(q):
+        cols, a = quarters[q], upper[q]
+        tsend[0, a, cols] = partial(3, q, a).astype(BF16)
+        return ring_copy(0, q, 0, a, rs_in, pair)
+
+    def send_first_next(q):
+        cols, b = quarters[q], lower[q]
+        tsend[0, b, cols] = partial(3, q, b).astype(BF16)
+        return ring_copy(1, q, 0, b, rs_in, next_pair)
 
     def own_parts(q):
         cols, a, b = quarters[q], upper[q], lower[q]
@@ -359,14 +364,14 @@
         tnear[b, cols] = partial(1, q, b)
         tfin[:, cols] = partial(0, q, pl.ds(0, ROWS))
 
-    def send_sum(q, first):
+    def send_sum(q):
         cols, a, b = quarters[q], upper[q], lower[q]
         with jax.named_scope(f"rs first wait {q}"):
-            first[0].wait_recv()
+            firsts_p[q].wait_recv()
         tsend[2, a, cols] = (tnear[a, cols] + rs_in[a, cols].astype(F32)).astype(BF16)
         one = ring_copy(0, q, 2, a, rs_n, next_pair)
         with jax.named_scope(f"rs first wait {q} b"):
-            first[1].wait_recv()
+            firsts_n[q].wait_recv()
         tsend[2, b, cols] = (tnear[b, cols] + rs_in[b, cols].astype(F32)).astype(BF16)
         return one, ring_copy(1, q, 2, b, rs_p, pair)
 
@@ -488,16 +493,18 @@
     with jax.named_scope("gh pair wait"):
         for copy in grad_pair:
             copy.wait_recv()
-    singles_p, firsts, summed = [], [], []
+    singles_p, firsts_p, firsts_n, summed = [], [], [], []
     with jax.named_scope("ring sums 0"):
         for r in (1, 3):
             grad_group(r)
-        firsts.append(send_first(0))
+        firsts_n.append(send_first_next(0))
+        firsts_p.append(send_first_pair(0))
         singles_p.append(send_single_pair(0))
     with jax.named_scope("ring sums 1"):
-        for q in (1, 2):
-            firsts.append(send_first(q))
-            singles_p.append(send_single_pair(q))
+        firsts_n.append(send_first_next(1))
+        firsts_p.append(send_first_pair(1))
+        singles_p.append(send_single_pair(1))
+        firsts_p.append(send_first_pair(2))
         for q in range(2 * NCH):
             own_parts(q)
     with jax.named_scope("f part wait"):
@@ -506,18 +513,20 @@
         for h in range(2):
             stack_up(0, 1, h, pair_total(0, half(1, h)) + fr[:, h * HALF:(h + 1) * HALF].astype(F32))
         give_back(0, 1)
-    summed.append(send_sum(0, firsts[0]))
-    summed.append(send_sum(1, firsts[1]))
-    with jax.named_scope("ring sums 3"):
+    for q in range(2):
+        summed.append(send_sum(q))
+    with jax.named_scope("first 2 3"):
+        firsts_n.append(send_first_next(2))
+        singles_p.append(send_single_pair(2))
         singles_n.append(send_single_next(2))
-        firsts.append(send_first(3))
-    summed.append(send_sum(2, firsts[2]))
-    with jax.named_scope("ring sums 4"):
-        singles_p.append(send_single_pair(3))
-        singles_n.append(send_single_next(3))
-    finish_sum(0)
-    summed.append(send_sum(3, firsts[3]))
-    finish_sum(1)
+        firsts_p.append(send_first_pair(3))
+        firsts_n.append(send_first_next(3))
+    for q in range(2):
+        finish_sum(q)
+    summed.append(send_sum(2))
+    singles_p.append(send_single_pair(3))
+    singles_n.append(send_single_next(3))
+    summed.append(send_sum(3))
     home_forward(0)
     finish_sum(2)
     home_forward(1)
@@ -547,7 +556,7 @@
     vmem = pl.BlockSpec(memory_space=pltpu.VMEM)
     hbm = pl.BlockSpec(memory_space=pl.ANY)
     dma = pltpu.SemaphoreType.DMA
-    out = jax.ShapeDtypeStruct((TOK, D), BF16)
+    out = pltpu.VMEM((TOK, D), BF16)
     scratch = [
         pltpu.VMEM((TOK, D), BF16),
         pltpu.VMEM((TOK, D), BF16),

time: 164 us -> 159 us (0.970)
  Pallas kernels: 160 us -> 156 us
    pallas_call x1, Pallas kernels: 160 us -> 156 us  [on_device(): call(forward_inputs[0], backward_cotangent[0], backward_inputs[0], row(fo...]
where the time goes in v5:
time: 159 us; the launch traced here: 158 us
  Pallas kernels  156 us (98%)
  local copies, waits for them, and re-layouts  1.85 us (1%)
    pallas_call x1, Pallas kernels, on_device(): call(forward_inputs[0], backward_cotangent[0], backward_inputs[0], row(fo...  156 us

profile of v5, /device:TPU:1, one launch (start us, length us, event | category | flops | bytes accessed | tf_op | source)
XLA Modules:
  0.0 158.4 jit_solution(13128037450108466553)
XLA Ops:
  0.6 155.9 %shard_map.131 = (bf16[128,3584]{1,0:T(8,128)(2,1)S(1)}, bf16[128,3584]{1,0:T(8,128)(2,1)S(1)}) custom-call(bf16[128,3584]{1,0:T(8,128)(2,1)} %bitcast.18, bf16[128,3584]{1,0:T(8,128)(2,1)} %bitcast.19, bf16[128,3584]{1,0:T(8,128)(2,1)} %bitcast.20, s32[1,128]{1,0:T(1,128)} %bitcast.22, f32[1,128]{1,0:T(1,128)} %bitcast.23, s32[1,128]{1,0:T(1,128)} %bitcast.24, ...), custom_call_target="tpu_custom_call" | custom-call | flops 10000000000 | bytes 20000000 | tf_op jit(solution)/shard_map/pallas_call | solution.py:617
  156.6 0.9 copy.16
  157.5 0.9 copy.17

commit v6 on v5

--- a/solution.py
+++ b/solution.py
@@ -329,7 +329,7 @@
         return nt(gj[r, rows, :HID], wg[cols, :]) + nt(gj[r, rows, HID:], wu[cols, :])
 
     quarters = [pl.ds(q * HALF, HALF) for q in range(2 * NCH)]
-    cut = [80, 80, 80, 96]
+    cut = [80, 80, 80, 80]
     upper = [pl.ds(0, n) for n in cut]
     lower = [pl.ds(n, ROWS - n) for n in cut]
 
@@ -386,28 +386,31 @@
         for j in range(NSUB):
             ys[i, c, j * ROWS:(j + 1) * ROWS, h * 128:(h + 1) * 128] = total[:, j * 128:(j + 1) * 128]
 
-    def give_back_quarter(q):
-        c, lanes = q // 2, pl.ds(q % 2 * 128, 128)
-        send[3, c, :, lanes] = nn(pack_m[...], ys[1, c, :, lanes]).astype(BF16)
+    def quarter_of(n):
+        return (3, 1, n // 2, pl.ds(n % 2 * 128, 128)) if n < 4 else (2, 0, 1, pl.ds(n % 2 * 128, 128))
+
+    def give_back_quarter(n):
+        i, y, c, lanes = quarter_of(n)
+        send[i, c, :, lanes] = nn(pack_m[...], ys[y, c, :, lanes]).astype(BF16)
+        own = pl.ds(pl.multiple_of(e * BLK, BLK), BLK)
 
         def one(d, carry):
             to = place(d)
             pltpu.make_async_remote_copy(
-                src_ref=send.at[3, c, pl.ds(pl.multiple_of(to * BLK, BLK), BLK), lanes],
-                dst_ref=recv.at[3, c, pl.ds(pl.multiple_of(e * BLK, BLK), BLK), lanes],
-                send_sem=b_send.at[q], recv_sem=b_recv.at[q],
+                src_ref=send.at[i, c, pl.ds(pl.multiple_of(to * BLK, BLK), BLK), lanes],
+                dst_ref=recv.at[i, c, own, lanes],
+                send_sem=b_send.at[n], recv_sem=b_recv.at[n],
                 device_id=(p, to * RING + k), device_id_type=MESH).start()
             return carry
         lax.fori_loop(1, NEXP, one, 0)
-        own = pl.ds(pl.multiple_of(e * BLK, BLK), BLK)
-        recv[3, c, own, lanes] = send[3, c, own, lanes]
-
-    def whole_quarter(q):
-        c, lanes = q // 2, pl.ds(q % 2 * 128, 128)
+        recv[i, c, own, lanes] = send[i, c, own, lanes]
+
+    def whole_quarter(n):
+        i, y, c, lanes = quarter_of(n)
         part = pl.ds(0, PACK - BLK)
         return pltpu.make_async_remote_copy(
-            src_ref=send.at[3, c, part, lanes], dst_ref=recv.at[3, c, part, lanes],
-            send_sem=b_send.at[q], recv_sem=b_recv.at[q], device_id=pair, device_id_type=MESH)
+            src_ref=send.at[i, c, part, lanes], dst_ref=recv.at[i, c, part, lanes],
+            send_sem=b_send.at[n], recv_sem=b_recv.at[n], device_id=pair, device_id_type=MESH)
 
     def pair_total(i, cols):
         return nn(hk[i], wd[0, :, cols]) + nn(hp[i], wd[1, :, cols])
@@ -421,7 +424,10 @@
         with jax.named_scope(f"home f wait {c}"):
             if c == 0:
                 pipe_f.wait_recv()
-            whole(2, c).wait_recv()
+                whole(2, 0).wait_recv()
+            else:
+                whole_quarter(4).wait_recv()
+                whole_quarter(5).wait_recv()
 
         def one(j, carry):
             got = nn(get_m[0, pl.ds(pl.multiple_of(j * TOK, TOK), TOK), :], recv[2, c])
@@ -485,11 +491,12 @@
             other = pl.ds(HID + i * (HID // 2), HID // 2)
             gsp[1, :, part] = (nt(xbn[...], wd[1, part, F2]) + gpn[:, other].astype(F32)).astype(BF16)
             grad_pair.append(remote(gsp.at[1, :, part], ghb.at[3, :, part], g_send.at[4 + i], g_recv.at[4 + i], pair))
+    f_parts = []
     with jax.named_scope("out f part"):
         for h in range(2):
             part = pl.ds(h * HALF, HALF)
             fs[:, part] = pair_total(1, half(1, h)).astype(BF16)
-        f_part = remote(fs, fr, h_send.at[4], h_recv.at[4], next_pair)
+            f_parts.append(remote(fs.at[:, part], fr.at[:, part], h_send.at[4 + h], h_recv.at[4 + h], next_pair))
     with jax.named_scope("gh pair wait"):
         for copy in grad_pair:
             copy.wait_recv()
@@ -505,14 +512,17 @@
         firsts_p.append(send_first_pair(1))
         singles_p.append(send_single_pair(1))
         firsts_p.append(send_first_pair(2))
-        for q in range(2 * NCH):
+        for q in range(2):
             own_parts(q)
-    with jax.named_scope("f part wait"):
-        f_part.wait_recv()
-    with jax.named_scope("out f 1"):
-        for h in range(2):
+    for h in range(2):
+        with jax.named_scope(f"f part wait {h}"):
+            f_parts[h].wait_recv()
+        with jax.named_scope(f"out f 1 {h}"):
             stack_up(0, 1, h, pair_total(0, half(1, h)) + fr[:, h * HALF:(h + 1) * HALF].astype(F32))
-        give_back(0, 1)
+            give_back_quarter(4 + h)
+            if h == 0:
+                own_parts(2)
+                own_parts(3)
     for q in range(2):
         summed.append(send_sum(q))
     with jax.named_scope("first 2 3"):
@@ -544,11 +554,10 @@
 
     for copy in pending:
         copy.wait_send()
-    for i in range(3):
-        for c in range(NCH):
-            whole(i, c).wait_send()
-    for q in range(2 * NCH):
-        whole_quarter(q).wait_send()
+    for i, c in ((0, 0), (0, 1), (1, 0), (1, 1), (2, 0)):
+        whole(i, c).wait_send()
+    for n in range(6):
+        whole_quarter(n).wait_send()
 
 
 def on_device(forward_inputs, forward_routes, forward_gates, backward_inputs, backward_cotangent, backward_routes,
@@ -598,7 +607,7 @@
         pltpu.VMEM((2, NCH, NSUB * ROWS, 256), BF16),
         pltpu.VMEM((TOK, D), F32),
         dma((6,)), dma((4,)), dma((4,)), dma((8,)), dma((8,)), dma((8,)), dma((8,)), dma((12,)), dma((12,)),
-        dma((5,)), dma((5,)), dma((6,)), dma((6,)), dma((24,)), dma((24,)), dma((4,)), dma((4,)),
+        dma((6,)), dma((6,)), dma((6,)), dma((6,)), dma((24,)), dma((24,)), dma((6,)), dma((6,)),
     ]
     call = pl.pallas_call(
         kernel,

time: 159 us -> 158 us (level)
  no operation moved by 1% of the time
where the time goes in v6:
time: 158 us; the launch traced here: 157 us
  Pallas kernels  155 us (98%)
  local copies, waits for them, and re-layouts  1.85 us (1%)
    pallas_call x1, Pallas kernels, on_device(): call(forward_inputs[0], backward_cotangent[0], backward_inputs[0], row(fo...  155 us

profile of v6, /device:TPU:1, one launch (start us, length us, event | category | flops | bytes accessed | tf_op | source)
XLA Modules:
  0.0 157.4 jit_solution(4517275256246882262)
XLA Ops:
  0.6 154.9 %shard_map.131 = (bf16[128,3584]{1,0:T(8,128)(2,1)S(1)}, bf16[128,3584]{1,0:T(8,128)(2,1)S(1)}) custom-call(bf16[128,3584]{1,0:T(8,128)(2,1)} %bitcast.18, bf16[128,3584]{1,0:T(8,128)(2,1)} %bitcast.19, bf16[128,3584]{1,0:T(8,128)(2,1)} %bitcast.20, s32[1,128]{1,0:T(1,128)} %bitcast.22, f32[1,128]{1,0:T(1,128)} %bitcast.23, s32[1,128]{1,0:T(1,128)} %bitcast.24, ...), custom_call_target="tpu_custom_call" | custom-call | flops 10000000000 | bytes 20000000 | tf_op jit(solution)/shard_map/pallas_call | solution.py:626
  155.6 0.9 copy.16
  156.5 0.9 copy.17
